TPU v7x, 32 devices: a whole 2x2x4 slice. The times are simulated.
32 devices in a mesh: wide: 8 (over y, x, core), narrow: 4 (over z).
Axes of the slice: x: 2, y: 2, z: 4, core: 2. Of those that a mesh axis runs over, the one named last changes fastest.
Arguments:
- target: bfloat16 [32768, 512], P(('wide', 'narrow')), may hold values from -6 to 6
- memory: bfloat16 [32768, 512], P(('wide', 'narrow')), may hold values from -6 to 6
- cotangent: bfloat16 [32768, 512], P(('wide', 'narrow')), may hold values from -6 to 6
- target_lengths: int32 [32, 27], P(('wide', 'narrow')), may hold values from 1 to 250, 1024 in all within a row
- source_lengths: int32 [32, 27], P(('wide', 'narrow')), may hold values from 1 to 250, 1024 in all within a row
- self_qkv: bfloat16 [512, 1536], P(('wide', 'narrow')), may hold values from -0.25 to 0.25
- self_out: bfloat16 [512, 512], P(('wide', 'narrow')), may hold values from -1 to 1
- self_bias: bfloat16 [3, 512], P(None, ('wide', 'narrow')), may hold values from -3 to 3
- cross_qkv: bfloat16 [512, 1536], P(('wide', 'narrow')), may hold values from -0.25 to 0.25
- cross_out: bfloat16 [512, 512], P(('wide', 'narrow')), may hold values from -1 to 1
- cross_bias: bfloat16 [3, 512], P(None, ('wide', 'narrow')), may hold values from -3 to 3
- ff_in: bfloat16 [512, 2048], P(('wide', 'narrow')), may hold values from -0.25 to 0.25
- ff_in_bias: bfloat16 [2048], P(('wide', 'narrow')), may hold values from -3 to 3
- ff_out: bfloat16 [2048, 512], P(('wide', 'narrow')), may hold values from -0.125 to 0.125
- ff_out_bias: bfloat16 [512], P(('wide', 'narrow')), may hold values from -3 to 3
- ln_gain: bfloat16 [3, 512], P(None, ('wide', 'narrow')), may hold values from 0.5 to 1.5
- ln_bias: bfloat16 [3, 512], P(None, ('wide', 'narrow')), may hold values from -3 to 3
Outputs:
- layer_output: bfloat16 [32768, 512], P(('wide', 'narrow'))
- target_grad: float32 [32768, 512], P(('wide', 'narrow'))
- memory_grad: float32 [32768, 512], P(('wide', 'narrow'))
- self_qkv_grad: float32 [512, 1536], P(('wide', 'narrow'))
- self_out_grad: float32 [512, 512], P(('wide', 'narrow'))
- self_bias_grad: float32 [3, 512], P(None, ('wide', 'narrow'))
- cross_qkv_grad: float32 [512, 1536], P(('wide', 'narrow'))
- cross_out_grad: float32 [512, 512], P(('wide', 'narrow'))
- cross_bias_grad: float32 [3, 512], P(None, ('wide', 'narrow'))
- ff_in_grad: float32 [512, 2048], P(('wide', 'narrow'))
- ff_in_bias_grad: float32 [2048], P(('wide', 'narrow'))
- ff_out_grad: float32 [2048, 512], P(('wide', 'narrow'))
- ff_out_bias_grad: float32 [512], P(('wide', 'narrow'))
- ln_gain_grad: float32 [3, 512], P(None, ('wide', 'narrow'))
- ln_bias_grad: float32 [3, 512], P(None, ('wide', 'narrow'))
Inputs may be any that keep to these rules, and one draw needn't show every extreme that they name: `target_lengths`: each row sums to 1024, and its largest entry is 250. `source_lengths`: each row sums to 1024, and its largest entry is 250.
All inputs are finite; a program needn't handle non-finite values.
Results may differ from a plain program's by a relative error of at most 0.02.
Values may be sent and summed in bfloat16 or wider, within the bound.
A program may use at most 192 MiB of HBM per device.

v0:
```python
import jax
import jax.numpy as jnp
from jax import lax
from jax.sharding import PartitionSpec as P

HEADS = 8
HEAD = 64


EPSILON = 1e-05
MASKED = -1e30


def layer_norm(summed, gain, shift):
    centre = summed - jnp.mean(summed, axis=-1, keepdims=True)
    spread = jnp.mean(centre * centre, axis=-1, keepdims=True)
    return centre * lax.rsqrt(spread + EPSILON) * gain + shift


def segment_ids(lengths, row_count):
    ending = jnp.cumsum(lengths)
    places = jnp.arange(row_count, dtype=jnp.int32)
    return jnp.sum((places[:, None] >= ending[None, :]).astype(jnp.int32), axis=1)


def contract_rows(left_side, right_side):
    return lax.dot_general(
        left_side, right_side, (((0,), (0,)), ((), ())), preferred_element_type=jnp.float32
    )


def contract_cols(left_side, right_side):
    return lax.dot_general(
        left_side, right_side, (((1,), (1,)), ((), ())), preferred_element_type=jnp.float32
    )


def split_heads(matrix):
    return matrix.reshape(matrix.shape[0], HEADS, HEAD).transpose(1, 0, 2)


def join_heads(matrix):
    return matrix.transpose(1, 0, 2).reshape(matrix.shape[1], HEADS * HEAD)


def block_allowed(row_seg, col_seg, first_row, block_rows, causal):
    rows_here = row_seg[first_row : first_row + block_rows]
    allowed = rows_here[:, None] == col_seg[None, :]
    if causal:
        row_place = jnp.arange(first_row, first_row + block_rows, dtype=jnp.int32)
        col_place = jnp.arange(col_seg.shape[0], dtype=jnp.int32)
        allowed = allowed & (col_place[None, :] <= row_place[:, None])
    return allowed


def attend(query, key_rows, value_rows, row_seg, col_seg, causal):
    score_scale = HEAD ** (-0.5)
    row_count = query.shape[0]
    block_rows = min(512, row_count)
    query_heads = split_heads(query)
    key_heads = split_heads(key_rows)
    value_heads = split_heads(value_rows)
    mixed_parts = []
    logsum_parts = []
    for first_row in range(0, row_count, block_rows):
        allowed = block_allowed(row_seg, col_seg, first_row, block_rows, causal)

        def one_head(pieces):
            query_part, key_part, value_part = pieces
            scores = (
                jnp.dot(query_part, key_part.T, preferred_element_type=jnp.float32) * score_scale
            )
            scores = jnp.where(allowed, scores, MASKED)
            row_max = jnp.max(scores, axis=1, keepdims=True)
            exponent = jnp.exp(scores - row_max)
            row_total = jnp.sum(exponent, axis=1, keepdims=True)
            probability = (exponent / row_total).astype(jnp.bfloat16)
            mixed_rows = jnp.dot(probability, value_part, preferred_element_type=jnp.float32)
            return (mixed_rows, (row_max + jnp.log(row_total))[:, 0])

        mixed_rows, logsum = lax.map(
            one_head, (query_heads[:, first_row : first_row + block_rows], key_heads, value_heads)
        )
        mixed_parts.append(mixed_rows)
        logsum_parts.append(logsum)
    return (join_heads(jnp.concatenate(mixed_parts, axis=1)), jnp.concatenate(logsum_parts, axis=1))


def attend_back(query, key_rows, value_rows, logsum, grad_mixed, row_seg, col_seg, causal):
    score_scale = HEAD ** (-0.5)
    row_count = query.shape[0]
    block_rows = min(512, row_count)
    query_heads = split_heads(query)
    key_heads = split_heads(key_rows)
    value_heads = split_heads(value_rows)
    grad_heads = split_heads(grad_mixed)
    query_grads = []
    key_grad = jnp.zeros(key_heads.shape, jnp.float32)
    value_grad = jnp.zeros(value_heads.shape, jnp.float32)
    for first_row in range(0, row_count, block_rows):
        allowed = block_allowed(row_seg, col_seg, first_row, block_rows, causal)

        def one_head(pieces):
            query_part, key_part, value_part, grad_part, logsum_part = pieces
            scores = (
                jnp.dot(query_part, key_part.T, preferred_element_type=jnp.float32) * score_scale
            )
            scores = jnp.where(allowed, scores, MASKED)
            probability = jnp.exp(scores - logsum_part[:, None])
            grad_prob = jnp.dot(grad_part, value_part.T, preferred_element_type=jnp.float32)
            correction = jnp.sum(probability * grad_prob, axis=1, keepdims=True)
            grad_score = (probability * (grad_prob - correction)).astype(jnp.bfloat16)
            query_term = (
                jnp.dot(grad_score, key_part, preferred_element_type=jnp.float32) * score_scale
            )
            key_term = contract_rows(grad_score, query_part) * score_scale
            value_term = contract_rows(probability.astype(jnp.bfloat16), grad_part)
            return (query_term, key_term, value_term)

        query_term, key_term, value_term = lax.map(
            one_head,
            (
                query_heads[:, first_row : first_row + block_rows],
                key_heads,
                value_heads,
                grad_heads[:, first_row : first_row + block_rows],
                logsum[:, first_row : first_row + block_rows],
            ),
        )
        query_grads.append(query_term)
        key_grad = key_grad + key_term
        value_grad = value_grad + value_term
    return (
        join_heads(jnp.concatenate(query_grads, axis=1)),
        join_heads(key_grad),
        join_heads(value_grad),
    )


def local(
    target,
    memory,
    cotangent,
    target_lengths,
    source_lengths,
    self_qkv,
    self_out,
    self_bias,
    cross_qkv,
    cross_out,
    cross_bias,
    ff_in,
    ff_in_bias,
    ff_out,
    ff_out_bias,
    ln_gain,
    ln_bias,
):
    model_width = self_out.shape[1]
    row_seg = segment_ids(target_lengths[0], target.shape[0])
    col_seg = segment_ids(source_lengths[0], memory.shape[0])
    s_qkv, s_out, s_bias, norm_gain, norm_shift = (
        lax.all_gather(self_qkv, ("wide", "narrow"), axis=0, tiled=True),
        lax.all_gather(self_out, ("wide", "narrow"), axis=0, tiled=True),
        lax.all_gather(self_bias, ("wide", "narrow"), axis=1, tiled=True),
        lax.all_gather(ln_gain, ("wide", "narrow"), axis=1, tiled=True),
        lax.all_gather(ln_bias, ("wide", "narrow"), axis=1, tiled=True),
    )
    gain_full = norm_gain.astype(jnp.float32)
    shift_full = norm_shift.astype(jnp.float32)
    s_bias_full = s_bias.astype(jnp.float32)
    packed = jnp.dot(target, s_qkv, preferred_element_type=jnp.float32)
    query = (packed[:, :model_width] + s_bias_full[0]).astype(jnp.bfloat16)
    key_rows = packed[:, model_width : 2 * model_width].astype(jnp.bfloat16)
    value_rows = (packed[:, 2 * model_width :] + s_bias_full[1]).astype(jnp.bfloat16)
    self_mix, self_logsum = attend(query, key_rows, value_rows, row_seg, row_seg, True)
    self_mix_low = self_mix.astype(jnp.bfloat16)
    residual_one = (
        target.astype(jnp.float32)
        + jnp.dot(self_mix_low, s_out, preferred_element_type=jnp.float32)
        + s_bias_full[2]
    )
    normed_one = layer_norm(residual_one, gain_full[0], shift_full[0])
    normed_one_low = normed_one.astype(jnp.bfloat16)
    c_qkv, c_out, c_bias = (
        lax.all_gather(cross_qkv, ("wide", "narrow"), axis=0, tiled=True),
        lax.all_gather(cross_out, ("wide", "narrow"), axis=0, tiled=True),
        lax.all_gather(cross_bias, ("wide", "narrow"), axis=1, tiled=True),
    )
    c_bias_full = c_bias.astype(jnp.float32)
    cross_query = (
        jnp.dot(normed_one_low, c_qkv[:, :model_width], preferred_element_type=jnp.float32)
        + c_bias_full[0]
    ).astype(jnp.bfloat16)
    memory_pack = jnp.dot(memory, c_qkv[:, model_width:], preferred_element_type=jnp.float32)
    cross_key = memory_pack[:, :model_width].astype(jnp.bfloat16)
    cross_value = (memory_pack[:, model_width:] + c_bias_full[1]).astype(jnp.bfloat16)
    cross_mix, cross_logsum = attend(cross_query, cross_key, cross_value, row_seg, col_seg, False)
    cross_mix_low = cross_mix.astype(jnp.bfloat16)
    residual_two = (
        normed_one
        + jnp.dot(cross_mix_low, c_out, preferred_element_type=jnp.float32)
        + c_bias_full[2]
    )
    normed_two = layer_norm(residual_two, gain_full[1], shift_full[1])
    normed_two_low = normed_two.astype(jnp.bfloat16)
    f_in, f_in_bias, f_out, f_out_bias = (
        lax.all_gather(ff_in, ("wide", "narrow"), axis=0, tiled=True),
        lax.all_gather(ff_in_bias, ("wide", "narrow"), axis=0, tiled=True),
        lax.all_gather(ff_out, ("wide", "narrow"), axis=0, tiled=True),
        lax.all_gather(ff_out_bias, ("wide", "narrow"), axis=0, tiled=True),
    )
    pre_act = jnp.dot(normed_two_low, f_in, preferred_element_type=jnp.float32) + f_in_bias.astype(
        jnp.float32
    )
    activated = jax.nn.gelu(pre_act).astype(jnp.bfloat16)
    residual_three = (
        normed_two
        + jnp.dot(activated, f_out, preferred_element_type=jnp.float32)
        + f_out_bias.astype(jnp.float32)
    )
    layer_output = layer_norm(residual_three, gain_full[2], shift_full[2]).astype(jnp.bfloat16)
    f_in, f_in_bias, f_out, f_out_bias, norm_gain, norm_shift = (
        lax.all_gather(ff_in, ("wide", "narrow"), axis=0, tiled=True),
        lax.all_gather(ff_in_bias, ("wide", "narrow"), axis=0, tiled=True),
        lax.all_gather(ff_out, ("wide", "narrow"), axis=0, tiled=True),
        lax.all_gather(ff_out_bias, ("wide", "narrow"), axis=0, tiled=True),
        lax.all_gather(ln_gain, ("wide", "narrow"), axis=1, tiled=True),
        lax.all_gather(ln_bias, ("wide", "narrow"), axis=1, tiled=True),
    )
    gain_full = norm_gain.astype(jnp.float32)
    shift_full = norm_shift.astype(jnp.float32)
    _, norm_back = jax.vjp(layer_norm, residual_three, gain_full[2], shift_full[2])
    grad_three, gain_three, shift_three = norm_back(cotangent.astype(jnp.float32))
    grad_three_low = grad_three.astype(jnp.bfloat16)
    f_out_grad = contract_rows(activated, grad_three_low)
    f_out_bias_grad = jnp.sum(grad_three, axis=0)
    grad_act = contract_cols(grad_three_low, f_out)
    _, gelu_back = jax.vjp(jax.nn.gelu, pre_act)
    grad_pre = gelu_back(grad_act)[0]
    grad_pre_low = grad_pre.astype(jnp.bfloat16)
    f_in_grad = contract_rows(normed_two_low, grad_pre_low)
    f_in_bias_grad = jnp.sum(grad_pre, axis=0)
    grad_two_in = grad_three + contract_cols(grad_pre_low, f_in)
    ffn_summed = (
        lax.psum_scatter(f_in_grad, ("wide", "narrow"), scatter_dimension=0, tiled=True),
        lax.psum_scatter(f_in_bias_grad, ("wide", "narrow"), scatter_dimension=0, tiled=True),
        lax.psum_scatter(f_out_grad, ("wide", "narrow"), scatter_dimension=0, tiled=True),
        lax.psum_scatter(f_out_bias_grad, ("wide", "narrow"), scatter_dimension=0, tiled=True),
    )
    c_qkv, c_out, c_bias = (
        lax.all_gather(cross_qkv, ("wide", "narrow"), axis=0, tiled=True),
        lax.all_gather(cross_out, ("wide", "narrow"), axis=0, tiled=True),
        lax.all_gather(cross_bias, ("wide", "narrow"), axis=1, tiled=True),
    )
    _, norm_back = jax.vjp(layer_norm, residual_two, gain_full[1], shift_full[1])
    grad_two, gain_two, shift_two = norm_back(grad_two_in)
    grad_two_low = grad_two.astype(jnp.bfloat16)
    c_out_grad = contract_rows(cross_mix_low, grad_two_low)
    grad_cross_mix = contract_cols(grad_two_low, c_out).astype(jnp.bfloat16)
    cross_dq, cross_dk, cross_dv = attend_back(
        cross_query, cross_key, cross_value, cross_logsum, grad_cross_mix, row_seg, col_seg, False
    )
    cross_dq_low = cross_dq.astype(jnp.bfloat16)
    cross_dkv_low = jnp.concatenate([cross_dk, cross_dv], axis=1).astype(jnp.bfloat16)
    c_qkv_grad = jnp.concatenate(
        [contract_rows(normed_one_low, cross_dq_low), contract_rows(memory, cross_dkv_low)], axis=1
    )
    c_bias_grad = jnp.stack(
        [jnp.sum(cross_dq, axis=0), jnp.sum(cross_dv, axis=0), jnp.sum(grad_two, axis=0)], axis=0
    )
    memory_grad = contract_cols(cross_dkv_low, c_qkv[:, model_width:])
    grad_one_in = grad_two + contract_cols(cross_dq_low, c_qkv[:, :model_width])
    cross_summed = (
        lax.psum_scatter(c_qkv_grad, ("wide", "narrow"), scatter_dimension=0, tiled=True),
        lax.psum_scatter(c_out_grad, ("wide", "narrow"), scatter_dimension=0, tiled=True),
        lax.psum_scatter(c_bias_grad, ("wide", "narrow"), scatter_dimension=1, tiled=True),
    )
    s_qkv, s_out, s_bias = (
        lax.all_gather(self_qkv, ("wide", "narrow"), axis=0, tiled=True),
        lax.all_gather(self_out, ("wide", "narrow"), axis=0, tiled=True),
        lax.all_gather(self_bias, ("wide", "narrow"), axis=1, tiled=True),
    )
    _, norm_back = jax.vjp(layer_norm, residual_one, gain_full[0], shift_full[0])
    grad_one, gain_one, shift_one = norm_back(grad_one_in)
    grad_one_low = grad_one.astype(jnp.bfloat16)
    s_out_grad = contract_rows(self_mix_low, grad_one_low)
    grad_self_mix = contract_cols(grad_one_low, s_out).astype(jnp.bfloat16)
    self_dq, self_dk, self_dv = attend_back(
        query, key_rows, value_rows, self_logsum, grad_self_mix, row_seg, row_seg, True
    )
    self_dqkv_low = jnp.concatenate([self_dq, self_dk, self_dv], axis=1).astype(jnp.bfloat16)
    s_qkv_grad = contract_rows(target, self_dqkv_low)
    s_bias_grad = jnp.stack(
        [jnp.sum(self_dq, axis=0), jnp.sum(self_dv, axis=0), jnp.sum(grad_one, axis=0)], axis=0
    )
    target_grad = grad_one + contract_cols(self_dqkv_low, s_qkv)
    gain_grad = jnp.stack([gain_one, gain_two, gain_three], axis=0)
    shift_grad = jnp.stack([shift_one, shift_two, shift_three], axis=0)
    self_summed = (
        lax.psum_scatter(s_qkv_grad, ("wide", "narrow"), scatter_dimension=0, tiled=True),
        lax.psum_scatter(s_out_grad, ("wide", "narrow"), scatter_dimension=0, tiled=True),
        lax.psum_scatter(s_bias_grad, ("wide", "narrow"), scatter_dimension=1, tiled=True),
        lax.psum_scatter(gain_grad, ("wide", "narrow"), scatter_dimension=1, tiled=True),
        lax.psum_scatter(shift_grad, ("wide", "narrow"), scatter_dimension=1, tiled=True),
    )
    f_in_sum, f_in_bias_sum, f_out_sum, f_out_bias_sum = ffn_summed
    c_qkv_sum, c_out_sum, c_bias_sum = cross_summed
    s_qkv_sum, s_out_sum, s_bias_sum, gain_sum, shift_sum = self_summed
    return (
        layer_output,
        target_grad,
        memory_grad,
        s_qkv_sum,
        s_out_sum,
        s_bias_sum,
        c_qkv_sum,
        c_out_sum,
        c_bias_sum,
        f_in_sum,
        f_in_bias_sum,
        f_out_sum,
        f_out_bias_sum,
        gain_sum,
        shift_sum,
    )


def solution(mesh):
    return jax.shard_map(
        local,
        mesh=mesh,
        in_specs=(
            P(("wide", "narrow"), None),
            P(("wide", "narrow"), None),
            P(("wide", "narrow"), None),
            P(("wide", "narrow"), None),
            P(("wide", "narrow"), None),
            P(("wide", "narrow"), None),
            P(("wide", "narrow"), None),
            P(None, ("wide", "narrow")),
            P(("wide", "narrow"), None),
            P(("wide", "narrow"), None),
            P(None, ("wide", "narrow")),
            P(("wide", "narrow"), None),
            P(("wide", "narrow")),
            P(("wide", "narrow"), None),
            P(("wide", "narrow")),
            P(None, ("wide", "narrow")),
            P(None, ("wide", "narrow")),
        ),
        out_specs=(
            P(("wide", "narrow"), None),
            P(("wide", "narrow"), None),
            P(("wide", "narrow"), None),
            P(("wide", "narrow"), None),
            P(("wide", "narrow"), None),
            P(None, ("wide", "narrow")),
            P(("wide", "narrow"), None),
            P(("wide", "narrow"), None),
            P(None, ("wide", "narrow")),
            P(("wide", "narrow"), None),
            P(("wide", "narrow")),
            P(("wide", "narrow"), None),
            P(("wide", "narrow")),
            P(None, ("wide", "narrow")),
            P(None, ("wide", "narrow")),
        ),
        check_vma=False,
    )
```

profile of v0, /device:TPU:0, one launch (start us, length us, event | category | flops | bytes accessed | tf_op | source)
XLA Modules:
  0.0 2218.2 jit_solution(10515489327330467818)
XLA Ops:
  16.8 69.9 %all-gather = bf16[32,16,3]{1,2,0:T(4,128)(2,1)S(1)} all-gather(bf16[1,16,3]{1,2,0:T(4,128)(2,1)S(1)} %bitcast.581), channel_id=1, replica_groups=mesh['wide'=8,'narrow'=4] {'wide','narrow'}, dimensions={0}, use_global_device_ids=true | all-gather | bytes 3168 | tf_op jit(solution)/shard_map/all_gather | solution.py:165
  87.4 74.2 %all_gather.45 = bf16[512,512]{1,0:T(8,128)(2,1)} all-gather(bf16[16,512]{1,0:T(8,128)(2,1)S(1)} %copy-done.46), channel_id=1, replica_groups=mesh['wide'=8,'narrow'=4] {'wide','narrow'}, dimensions={0}, use_global_device_ids=true | all-gather | bytes 540672 | tf_op jit(solution)/shard_map/all_gather | solution.py:164
  162.9 64.4 %all-gather.1 = bf16[32,16,3]{1,2,0:T(4,128)(2,1)S(1)} all-gather(bf16[1,16,3]{1,2,0:T(4,128)(2,1)S(1)} %bitcast.582), channel_id=1, replica_groups=mesh['wide'=8,'narrow'=4] {'wide','narrow'}, dimensions={0}, use_global_device_ids=true | all-gather | bytes 3168 | tf_op jit(solution)/shard_map/all_gather | solution.py:166
  227.7 64.8 %all-gather.2 = bf16[32,16,3]{1,2,0:T(4,128)(2,1)S(1)} all-gather(bf16[1,16,3]{1,2,0:T(4,128)(2,1)S(1)} %bitcast.583), channel_id=1, replica_groups=mesh['wide'=8,'narrow'=4] {'wide','narrow'}, dimensions={0}, use_global_device_ids=true | all-gather | bytes 3168 | tf_op jit(solution)/shard_map/all_gather | solution.py:167
  292.8 64.4 %all-gather.3 = bf16[32,16,3]{1,2,0:T(4,128)(2,1)S(1)} all-gather(bf16[1,16,3]{1,2,0:T(4,128)(2,1)S(1)} %bitcast.584), channel_id=1, replica_groups=mesh['wide'=8,'narrow'=4] {'wide','narrow'}, dimensions={0}, use_global_device_ids=true | all-gather | bytes 3168 | tf_op jit(solution)/shard_map/all_gather | solution.py:188
  357.9 74.3 %all_gather.50 = bf16[512,512]{1,0:T(8,128)(2,1)} all-gather(bf16[16,512]{1,0:T(8,128)(2,1)S(1)} %copy-done.47), channel_id=1, replica_groups=mesh['wide'=8,'narrow'=4] {'wide','narrow'}, dimensions={0}, use_global_device_ids=true | all-gather | bytes 540672 | tf_op jit(solution)/shard_map/all_gather | solution.py:187
  432.6 38.2 %all-reduce.5 = (bf16[512]{0:T(512)(128)(2,1)S(1)}, bf16[2048]{0:T(1024)(128)(2,1)S(1)}) all-reduce(bf16[512]{0:T(512)(128)(2,1)S(1)} %dynamic-update-slice.1, bf16[2048]{0:T(1024)(128)(2,1)S(1)} %dynamic-update-slice), channel_id=1, replica_groups=mesh['wide'=8,'narrow'=4] {'wide','narrow'}, use_global_device_ids=true, to_apply=%add.1 | all-reduce | flops 2560 | bytes 10240
  488.0 35.9 %while.113 = (s32[]{:T(128)}, bf16[8,512,64]{1,2,0:T(8,128)(2,1)}, f32[8,512]{1,0:T(8,128)S(1)}, bf16[8,512,64]{2,1,0:T(8,128)(2,1)}, bf16[8,1024,64]{2,1,0:T(8,...) while((s32[]{:T(128)}, bf16[8,512,64]{1,2,0:T(8,128)(2,1)}, ...), condition=%wide.region_9.10_spmd.clone, body=%wide.region_6.9_spmd.clone.sunk | while | flops 139984384 | bytes 7108721 | solution.py:81
  526.4 34.6 %while.112 = (s32[]{:T(128)}, bf16[8,512,64]{1,2,0:T(8,128)(2,1)}, f32[8,512]{1,0:T(8,128)S(1)}, bf16[8,512,64]{2,1,0:T(8,128)(2,1)}, bf16[8,1024,64]{2,1,0:T(8,...) while((s32[]{:T(128)}, bf16[8,512,64]{1,2,0:T(8,128)(2,1)}, ...), condition=%wide.region_5.6_spmd.clone, body=%wide.region_2.0_spmd.clone.sunk | while | flops 139984384 | bytes 7106665 | solution.py:81
  578.4 34.4 %while.114 = (s32[]{:T(128)}, bf16[8,512,64]{1,2,0:T(8,128)(2,1)}, f32[8,512]{1,0:T(8,128)S(1)}, bf16[8,512,64]{2,1,0:T(8,128)(2,1)}, bf16[8,1024,64]{2,1,0:T(8,...) while((s32[]{:T(128)}, bf16[8,512,64]{1,2,0:T(8,128)(2,1)}, ...), condition=%wide.region_17.18_spmd.clone, body=%wide.region_14.17_spmd.clone.sunk | while | flops 138935808 | bytes 7106665 | solution.py:81
  612.8 34.5 %while.115 = (s32[]{:T(128)}, bf16[8,512,64]{1,2,0:T(8,128)(2,1)}, f32[8,512]{1,0:T(8,128)S(1)}, bf16[8,512,64]{2,1,0:T(8,128)(2,1)}, bf16[8,1024,64]{2,1,0:T(8,...) while((s32[]{:T(128)}, bf16[8,512,64]{1,2,0:T(8,128)(2,1)}, ...), condition=%wide.region_21.22_spmd.clone, body=%wide.region_18.21_spmd.clone.sunk | while | flops 138935808 | bytes 7106665 | solution.py:81
  652.9 8.1 fusion.206
  660.9 8.6 fusion.227
  674.1 8.2 fusion.228
  698.5 76.7 %while.116 = (s32[]{:T(128)}, f32[8,512,64]{1,2,0:T(8,128)}, f32[8,1024,64]{1,2,0:T(8,128)}, f32[8,1024,64]{1,2,0:T(8,128)}, bf16[8,512,64]{2,1,0:T(8,128)(2,1)}...) while((s32[]{:T(128)}, f32[8,512,64]{1,2,0:T(8,128)}, ...), condition=%wide.region_32.33_spmd.clone, body=%wide.region_30.32_spmd.clone.sunk | while | flops 340884992 | bytes 17716344 | solution.py:120
  779.4 76.8 %while.117 = (s32[]{:T(128)}, f32[8,512,64]{1,2,0:T(8,128)}, f32[8,1024,64]{1,2,0:T(8,128)}, f32[8,1024,64]{1,2,0:T(8,128)}, bf16[8,512,64]{2,1,0:T(8,128)(2,1)}...) while((s32[]{:T(128)}, f32[8,512,64]{1,2,0:T(8,128)}, ...), condition=%wide.region_35.36_spmd.clone, body=%wide.region_33.35_spmd.clone.sunk | while | flops 340884992 | bytes 17716344 | solution.py:120
  871.4 78.4 %while.119 = (s32[]{:T(128)}, f32[8,512,64]{1,2,0:T(8,128)}, f32[8,1024,64]{1,2,0:T(8,128)}, f32[8,1024,64]{1,2,0:T(8,128)S(1)}, bf16[8,512,64]{2,1,0:T(8,128)(2...) while((s32[]{:T(128)}, f32[8,512,64]{1,2,0:T(8,128)}, ...), condition=%wide.region_43.44_spmd.clone, body=%wide.region_41.43_spmd.clone.sunk | while | flops 341933568 | bytes 17718400 | solution.py:120
  954.1 75.3 %while.118 = (s32[]{:T(128)}, f32[8,512,64]{1,2,0:T(8,128)}, f32[8,1024,64]{1,2,0:T(8,128)}, f32[8,1024,64]{1,2,0:T(8,128)S(1)}, bf16[8,512,64]{2,1,0:T(8,128)(2...) while((s32[]{:T(128)}, f32[8,512,64]{1,2,0:T(8,128)}, ...), condition=%wide.region_40.41_spmd.clone, body=%wide.region_38.40_spmd.clone.sunk | while | flops 341933568 | bytes 17716344 | solution.py:120
  1077.0 9.8 fusion.195
  1088.4 6.7 fusion.177
  1096.8 5.5 add_add_fusion.6
  1107.8 40.1 %all-reduce.4 = (f32[2048]{0:T(1024)S(1)}, f32[512]{0:T(512)S(1)}) all-reduce(f32[2048]{0:T(1024)S(1)} %copy-done.54, f32[512]{0:T(512)S(1)} %add_reduce_fusion.2), channel_id=9, replica_groups=mesh['wide'=8,'narrow'=4] {'wide','narrow'}, use_global_device_ids=true, to_apply=%region_58.59.clone | all-reduce | flops 2560 | bytes 20480
  1149.0 4.5 fusion.189
  1154.8 13.3 reduce-scatter.39.cloned.1.call-done
  1169.5 130.7 %reduce-scatter.37.cloned.1.call-done = f32[16,3]{1,0:T(8,128)} async-done(((f32[512,3]{1,0:T(8,128)}), f32[16,3]{1,0:T(8,128)}) %reduce-scatter.37.cloned.1.call-update) | async-done | bytes 208
  1301.5 130.9 %reduce-scatter.33.cloned.1.call-done = f32[16,3]{1,0:T(8,128)} async-done(((f32[512,3]{1,0:T(8,128)}), f32[16,3]{1,0:T(8,128)}) %reduce-scatter.33.cloned.1.call-update) | async-done | bytes 208
  1433.8 132.9 %reduce-scatter.25.cloned.1.call-done = f32[16,512]{1,0:T(8,128)} async-done(((f32[512,512]{1,0:T(8,128)}), f32[16,512]{1,0:T(8,128)}) %reduce-scatter.25.cloned.1.call-update) | async-done | bytes 32784 | tf_op jit(solution)/shard_map/reduce_scatter | solution.py:276
  1566.7 134.5 %reduce-scatter.23.cloned.1.call-done = f32[16,512]{1,0:T(8,128)} async-done(((f32[512,512]{1,0:T(8,128)}), f32[16,512]{1,0:T(8,128)}) %reduce-scatter.23.cloned.1.call-update) | async-done | bytes 32784 | tf_op jit(solution)/shard_map/reduce_scatter | solution.py:302
  1701.2 103.9 %reduce-scatter.35.cloned.1.call-done = f32[16,1536]{1,0:T(8,128)} async-done(((f32[512,1536]{1,0:T(8,128)}), f32[16,1536]{1,0:T(8,128)}) %reduce-scatter.35.cloned.1.call-update) | async-done | bytes 98320
  1805.1 106.4 %reduce-scatter.31.cloned.1.call-done = f32[16,1536]{1,0:T(8,128)} async-done(((f32[512,1536]{1,0:T(8,128)}), f32[16,1536]{1,0:T(8,128)}) %reduce-scatter.31.cloned.1.call-update) | async-done | bytes 98320
  1911.5 150.0 %reduce-scatter.29.cloned.1.call-done = f32[64,512]{1,0:T(8,128)} async-done(((f32[2048,512]{1,0:T(8,128)}), f32[64,512]{1,0:T(8,128)}) %reduce-scatter.29.cloned.1.call-update) | async-done | bytes 131088 | tf_op jit(solution)/shard_map/reduce_scatter | solution.py:248
  2061.5 149.7 %reduce-scatter.27.cloned.1.call-done = f32[16,2048]{1,0:T(8,128)} async-done(((f32[512,2048]{1,0:T(8,128)}), f32[16,2048]{1,0:T(8,128)}) %reduce-scatter.27.cloned.1.call-update) | async-done | bytes 131088 | tf_op jit(solution)/shard_map/reduce_scatter | solution.py:246
  (710 shorter events, 607.6 us)
Async XLA Ops:
  7.2 565.2 %copy-start = (bf16[1024,512]{1,0:T(8,128)(2,1)S(1)}, bf16[1024,512]{1,0:T(8,128)(2,1)}, u32[]{:S(2)}) copy-start(bf16[1024,512]{1,0:T(8,128)(2,1)} %param.34) | copy-start | bytes 3145732
  7.2 9.6 copy-start.62
  7.2 79.8 %copy-start.66 = (s32[1,27]{1,0:T(1,128)S(1)}, s32[1,27]{1,0:T(1,128)}, u32[]{:S(2)}) copy-start(s32[1,27]{1,0:T(1,128)} %param.36) | copy-start | bytes 328
  7.2 80.2 %copy-start.46 = (bf16[16,512]{1,0:T(8,128)(2,1)S(1)}, bf16[16,512]{1,0:T(8,128)(2,1)}, u32[]{:S(2)}) copy-start(bf16[16,512]{1,0:T(8,128)(2,1)} %param.39) | copy-start | bytes 49156
  7.2 465.0 %all-gather.9.cloned.1.call-start = ((), (), s32[]{:S(2)}) async-start(), calls=%async_computation.10 | async-start | bytes 1622016 | tf_op jit(solution)/shard_map/all_gather | solution.py:163
  8.0 557.4 %all-gather.11.cloned.1.call-start = ((), (), s32[]{:S(2)}) async-start(), calls=%async_computation.11 | async-start | bytes 1622016 | tf_op jit(solution)/shard_map/all_gather | solution.py:186
  8.7 644.2 %all-gather.13.cloned.1.call-start = ((), (), s32[]{:S(2)}) async-start(), calls=%async_computation.12 | async-start | bytes 2162688 | tf_op jit(solution)/shard_map/all_gather | solution.py:208
  9.4 651.5 %all-gather.15.cloned.1.call-start = ((), (), s32[]{:S(2)}) async-start(), calls=%async_computation.13 | async-start | bytes 2162688 | tf_op jit(solution)/shard_map/all_gather | solution.py:210
  10.0 1143.4 %reduce-scatter.41.cloned.1.call-start = ((), (), s32[]{:S(2)}) async-start(), calls=%async_computation.23 | async-start | bytes 270336
  10.9 150.7 %copy-start.28 = (bf16[1024,512]{1,0:T(8,128)(2,1)S(1)}, bf16[1024,512]{1,0:T(8,128)(2,1)}, u32[]{:S(2)}) copy-start(bf16[1024,512]{1,0:T(8,128)(2,1)} %param.33) | copy-start | bytes 3145732
  14.8 148.2 %copy-start.63 = (bf16[3,16]{1,0:T(4,128)(2,1)S(1)}, bf16[3,16]{1,0:T(4,128)(2,1)}, u32[]{:S(2)}) copy-start(bf16[3,16]{1,0:T(4,128)(2,1)} %param.48) | copy-start | bytes 292
  14.8 212.9 %copy-start.64 = (bf16[3,16]{1,0:T(4,128)(2,1)S(1)}, bf16[3,16]{1,0:T(4,128)(2,1)}, u32[]{:S(2)}) copy-start(bf16[3,16]{1,0:T(4,128)(2,1)} %param.49) | copy-start | bytes 292
  14.8 278.0 %copy-start.65 = (bf16[3,16]{1,0:T(4,128)(2,1)S(1)}, bf16[3,16]{1,0:T(4,128)(2,1)}, u32[]{:S(2)}) copy-start(bf16[3,16]{1,0:T(4,128)(2,1)} %param.43) | copy-start | bytes 292
  14.8 342.7 %copy-start.67 = (s32[1,27]{1,0:T(1,128)S(1)}, s32[1,27]{1,0:T(1,128)}, u32[]{:S(2)}) copy-start(s32[1,27]{1,0:T(1,128)} %param.37) | copy-start | bytes 328
  14.8 343.0 %copy-start.47 = (bf16[16,512]{1,0:T(8,128)(2,1)S(1)}, bf16[16,512]{1,0:T(8,128)(2,1)}, u32[]{:S(2)}) copy-start(bf16[16,512]{1,0:T(8,128)(2,1)} %param.42) | copy-start | bytes 49156
  16.7 415.4 %copy-start.70 = (bf16[64]{0:T(256)(128)(2,1)S(1)}, bf16[64]{0:T(256)(128)(2,1)}, u32[]{:S(2)}) copy-start(bf16[64]{0:T(256)(128)(2,1)} %param.45) | copy-start | bytes 388
  16.7 415.6 %copy-start.71 = (bf16[16]{0:T(256)(128)(2,1)S(1)}, bf16[16]{0:T(256)(128)(2,1)}, u32[]{:S(2)}) copy-start(bf16[16]{0:T(256)(128)(2,1)} %param.47) | copy-start | bytes 100
  86.7 384.2 %copy-start.27 = (bf16[1024,512]{1,0:T(8,128)(2,1)S(1)}, bf16[1024,512]{1,0:T(8,128)(2,1)}, u32[]{:S(2)}) copy-start(bf16[1024,512]{1,0:T(8,128)(2,1)} %param.35) | copy-start | bytes 3145732
  227.6 457.8 %copy-start.52 = (f32[1,512]{1,0:T(1,128)}, f32[1,512]{1,0:T(1,128)S(1)}, u32[]{:S(2)}) copy-start(f32[1,512]{1,0:T(1,128)S(1)} %get-tuple-element.1035) | copy-start | bytes 6148
  292.8 368.2 %copy-start.60 = (f32[1,512]{1,0:T(1,128)}, f32[1,512]{1,0:T(1,128)S(1)}, u32[]{:S(2)}) copy-start(f32[1,512]{1,0:T(1,128)S(1)} %get-tuple-element.1038) | copy-start | bytes 6148
  470.9 203.1 %copy-start.55 = (f32[2048]{0:T(1024)}, f32[2048]{0:T(1024)S(1)}, u32[]{:S(2)}) copy-start(f32[2048]{0:T(1024)S(1)} %convert_element_type.150) | copy-start | bytes 24580
  651.2 34.2 %copy-start.42 = (f32[1024]{0:T(1024)}, f32[1024]{0:T(1024)S(1)}, u32[]{:S(2)}) copy-start(f32[1024]{0:T(1024)S(1)} %broadcast_multiply_fusion.1) | copy-start | bytes 12292
  652.8 32.6 %copy-start.50 = (f32[1024]{0:T(1024)}, f32[1024]{0:T(1024)S(1)}, u32[]{:S(2)}) copy-start(f32[1024]{0:T(1024)S(1)} %fusion.199) | copy-start | bytes 12292
  864.7 303.5 %reduce-scatter.39.cloned.1.call-start = ((), (), s32[]{:S(2)}) async-start(), calls=%async_computation.22 | async-start | bytes 270336
  1034.6 265.6 %reduce-scatter.37.cloned.1.call-start = ((), (), s32[]{:S(2)}) async-start(), calls=%async_computation.21 | async-start | bytes 270336
  1039.3 393.1 %reduce-scatter.33.cloned.1.call-start = ((), (), s32[]{:S(2)}) async-start(), calls=%async_computation.19 | async-start | bytes 270336
  1040.3 526.4 %reduce-scatter.25.cloned.1.call-start = ((), (), s32[]{:S(2)}) async-start(), calls=%async_computation.15 | async-start | bytes 1081344 | tf_op jit(solution)/shard_map/reduce_scatter | solution.py:276
  1044.0 657.1 %reduce-scatter.23.cloned.1.call-start = ((), (), s32[]{:S(2)}) async-start(), calls=%async_computation.14 | async-start | bytes 1081344 | tf_op jit(solution)/shard_map/reduce_scatter | solution.py:302
  1047.8 757.3 %reduce-scatter.35.cloned.1.call-start = ((), (), s32[]{:S(2)}) async-start(), calls=%async_computation.20 | async-start | bytes 3244032
  1061.4 850.1 %reduce-scatter.31.cloned.1.call-start = ((), (), s32[]{:S(2)}) async-start(), calls=%async_computation.18 | async-start | bytes 3244032
  1075.4 986.1 %reduce-scatter.29.cloned.1.call-start = ((), (), s32[]{:S(2)}) async-start(), calls=%async_computation.17 | async-start | bytes 4325376 | tf_op jit(solution)/shard_map/reduce_scatter | solution.py:248
  1086.9 1124.4 %reduce-scatter.27.cloned.1.call-start = ((), (), s32[]{:S(2)}) async-start(), calls=%async_computation.16 | async-start | bytes 4325376 | tf_op jit(solution)/shard_map/reduce_scatter | solution.py:246
  (56 other events, 141.8 us)
Sparse Core Ops, SparseCore 0:
  10.9 57.7 all-gather.8
  71.6 54.4 all-gather.10
  129.1 55.4 all-gather.12
  187.4 55.3 all-gather.14
  864.8 133.2 reduce-scatter.40
  1034.8 133.3 reduce-scatter.38
  1170.4 129.7 reduce-scatter.36
  1302.5 129.9 reduce-scatter.32
  1435.3 131.3 reduce-scatter.24
  1569.5 131.6 reduce-scatter.22
  1707.2 97.8 reduce-scatter.34
  1811.0 100.4 reduce-scatter.30
  1914.4 147.1 reduce-scatter.28
  2064.3 146.9 reduce-scatter.26
where the time goes:
time: 2230 us; the launch traced here: 2220 us
  waiting for transfers between devices  1060 us (48%)
  matrix products  493 us (22%)
  blocking collectives  490 us (22%)
  local copies, waits for them, and re-layouts  109 us (5%)
  other arithmetic  53.3 us (2%)
    unnamed x20, waiting for transfers between devices  488 us
    reduce_scatter x1, waiting for transfers between devices, local(): lax.psum_scatter(f_out_grad, ('wide', 'narrow'), scatter_dimension=0, til...  150 us
    reduce_scatter x1, waiting for transfers between devices, local(): lax.psum_scatter(f_in_grad, ('wide', 'narrow'), scatter_dimension=0, tile...  150 us
    dot_general x71, matrix products, contract_rows(): lax.dot_general(left_side, right_side, (((0,), (0,)), ((), ())), preferre...  145 us
    reduce_scatter x1, waiting for transfers between devices, local(): lax.psum_scatter(s_out_grad, ('wide', 'narrow'), scatter_dimension=0, til...  134 us
    reduce_scatter x1, waiting for transfers between devices, local(): lax.psum_scatter(c_out_grad, ('wide', 'narrow'), scatter_dimension=0, til...  133 us
    dot_general x64, matrix products, one_head(): jnp.dot(query_part, key_part.T, preferred_element_type=jnp.float32)  112 us
    unnamed x2, blocking collectives  78.3 us
  transfers between devices with their start and end apart: 14, of which 9 were waited for; matrix products, arithmetic and copies ran while one was open for 20% of the time, Pallas kernels for 0%

commit v1 on v0

v1 whole, which is shorter than its diff:
```python
import functools
import math

import jax
import jax.numpy as jnp
from jax import lax
from jax.experimental import pallas as pl
from jax.experimental.pallas import tpu as pltpu
from jax.sharding import PartitionSpec as P

HEADS = 8
HEAD = 64
PAIRS = HEADS // 2
PAIR = 2 * HEAD
EPSILON = 1e-05
MASKED = -1e30
LINE = 128
TILE = 512
CHUNK = 512
VECTORS = 24
F32 = jnp.float32
BF16 = jnp.bfloat16
MESH = pl.DeviceIdType.MESH
VMEM_BYTES = 63 * 1024 * 1024

SELF_BIAS, CROSS_BIAS, GAIN, SHIFT, OUT_BIAS, IN_BIAS = 0, 3, 6, 9, 12, 13


def nn(left_side, right_side):
    return lax.dot_general(
        left_side, right_side, (((1,), (0,)), ((), ())), preferred_element_type=F32
    )


def nt(left_side, right_side):
    return lax.dot_general(
        left_side, right_side, (((1,), (1,)), ((), ())), preferred_element_type=F32
    )


def tn(left_side, right_side):
    return lax.dot_general(
        left_side, right_side, (((0,), (0,)), ((), ())), preferred_element_type=F32
    )


def part(step, size):
    if isinstance(step, int):
        return slice(step * size, (step + 1) * size)
    return pl.ds(pl.multiple_of(step * size, size), size)


def matrix(ref, first=0, columns=None):
    columns = ref.shape[-1] if columns is None else columns
    value = ref[:, :, :, :, first : first + columns]
    return value.reshape(-1, columns)


def loop(count, body, hooks=(), shift=0):
    def step(i, carry):
        body(i)
        for place, move in hooks:
            pl.when(i + shift == place)(move)
        return carry

    lax.fori_loop(0, count, step, 0)


def each(count, body):
    for i in range(count):
        body(i)


def hook(every, place, *moves):
    def move():
        for group, step in moves:
            every(group, step)

    return [(place, move)] if every is not None else []


def normalise(summed):
    centre = summed - jnp.mean(summed, axis=-1, keepdims=True)
    spread = jnp.mean(centre * centre, axis=-1, keepdims=True)
    scale = lax.rsqrt(spread + EPSILON)
    return centre * scale, scale


def normalise_back(grad, hat, scale, gain):
    inner = grad * gain
    first = jnp.mean(inner, axis=-1, keepdims=True)
    second = jnp.mean(inner * hat, axis=-1, keepdims=True)
    return (inner - first - hat * second) * scale


def column_sum(value):
    return jnp.sum(value, axis=0, keepdims=True)


def sentence_hits(lengths, rows):
    lane = lax.broadcasted_iota(jnp.int32, (1, LINE), 1)
    first = jnp.zeros((1, LINE), jnp.int32)
    last = jnp.zeros((1, LINE), jnp.int32)
    total = jnp.int32(0)
    for s in range(lengths.shape[1]):
        first = jnp.where(lane == s, total, first)
        total = total + lengths[0, s]
        last = jnp.where(lane == s, total, last)
    row = lax.broadcasted_iota(jnp.int32, (rows, LINE), 0)
    return (row >= first) & (row < last)


def twice(row):
    return jnp.concatenate([row, row], axis=1)


def beside(left_side, right_side):
    return jnp.concatenate([left_side, right_side], axis=1)


def stacked(value):
    lane = lax.broadcasted_iota(jnp.int32, (1, PAIR), 1)
    left = (lane < HEAD).astype(BF16)
    right = (lane >= HEAD).astype(BF16)
    return jnp.concatenate([value * left, value * right], axis=0)


def pair_row(ref, block, pair):
    return jnp.concatenate(
        [ref[block, pl.ds(2 * pair, 1), :], ref[block, pl.ds(2 * pair + 1, 1), :]], axis=1
    )


def diagonal(value):
    return jnp.concatenate([value[:HEAD, :LINE], value[HEAD:, LINE:]], axis=0)


def spread_rows(row):
    return jnp.concatenate(
        [
            jnp.broadcast_to(row[:, :LINE], (HEAD, LINE)),
            jnp.broadcast_to(row[:, LINE:], (HEAD, LINE)),
        ],
        axis=0,
    )


def keep_row(ref, block, pair, row):
    ref[block, pl.ds(2 * pair, 1), :] = row[:, :LINE]
    ref[block, pl.ds(2 * pair + 1, 1), :] = row[:, LINE:]


def score_back(probability, value_part, grad_block, delta):
    grad_prob = nt(value_part, grad_block) - delta
    return probability * grad_prob.astype(BF16)


def write_grad(grad_ref, delta_ref, portion, tile, grad_low, mixed_low):
    product = grad_low.astype(F32) * mixed_low.astype(F32)
    shape = (2 * HEADS, product.shape[1])
    head = lax.broadcasted_iota(jnp.int32, shape, 0) % HEADS
    owner = lax.broadcasted_iota(jnp.int32, shape, 1) // HEAD
    chosen = (head == owner).astype(BF16)
    high = product.astype(BF16)
    rest = (product - high.astype(F32)).astype(BF16)
    delta = (nt(chosen, high) + nt(chosen, rest))[:HEADS]
    for n in range(TILE // LINE):
        lines = slice(n * LINE, (n + 1) * LINE)
        block = tile * (TILE // LINE) + n
        by = portion[block]
        delta_ref[block] = delta[:, lines] * by
        high = by.astype(BF16)
        rest = (by - high.astype(F32)).astype(BF16)
        wide = tn(jnp.concatenate([high, rest], axis=0), chosen)
        grad_ref[part(block, LINE), :] = (grad_low[lines].astype(F32) * wide).astype(BF16)


def weight_grad(out_ref, left_ref, right_ref, first=0, start=0, count=None):
    rows = left_ref.shape[1]
    columns = right_ref.shape[1] if count is None else count
    wide = min(columns, CHUNK)
    piece = CHUNK
    blocks = out_ref.shape[3]

    def step(i):
        turned = left_ref[:, part(i, piece)].T

        def column(j):
            right = right_ref[:, pl.ds(pl.multiple_of(start + j * wide, LINE), wide)]
            value = nn(turned, right).astype(BF16)
            lanes = pl.ds(pl.multiple_of(first + j * wide, LINE), wide)
            if rows == piece:
                out_ref[:, :, :, :, lanes] = value.reshape(2, 2, 2, blocks, wide)
            else:
                out_ref[i // 2, i % 2, :, :, lanes] = value.reshape(2, blocks, wide)

        loop(columns // wide, column)

    loop(rows // piece, step)


class Copies:
    COUNT = 128

    def __init__(self, sems):
        self.sems, self.used, self.open = sems, 0, {}

    def start(self, source, target):
        number = self.used
        self.used += 1
        self.open[number] = pltpu.make_async_copy(source, target, self.sems.at[number])
        self.open[number].start()
        return number

    def tiles(self, source, target, count, size):
        return Tiles(self, source, target, count, size)

    def wait(self, *numbers):
        for number in numbers:
            if number in self.open:
                self.open.pop(number).wait()

    def close(self):
        self.wait(*list(self.open))


class Tiles:
    def __init__(self, owner, source, target, count, size):
        self.source, self.target, self.size, self.count = source, target, size, count
        self.sems, self.first = owner.sems, owner.used
        owner.used += count

    def copy(self, i):
        lines = part(i, self.size)
        return pltpu.make_async_copy(
            self.source.at[lines], self.target.at[lines], self.sems.at[self.first + i]
        )

    def start(self, i):
        self.copy(i).start()

    def start_all(self):
        for i in range(self.count):
            self.start(i)

    def wait(self, i):
        self.copy(i).wait()

    def wait_all(self):
        for i in range(self.count):
            self.wait(i)


class Kept:
    SLOTS = 2

    def __init__(self, owner, far_ref, made, back):
        self.far, self.made, self.back = far_ref, made, back
        self.count, self.rows, self.lanes = far_ref.shape
        self.sems, self.out, self.into = owner.sems, owner.used, owner.used + self.count
        owner.used += 2 * self.count

    def place(self, t, p=0, lanes=2 * LINE):
        start = t % self.SLOTS * (self.made.shape[1] // self.SLOTS) + p * 2 * LINE
        return pl.ds(pl.multiple_of(start, 2 * LINE), lanes)

    def slot(self, buffer, t):
        return buffer.at[pl.ds(0, self.rows), self.place(t, 0, self.lanes)]

    def leaving(self, t):
        return pltpu.make_async_copy(
            self.slot(self.made, t), self.far.at[t], self.sems.at[self.out + t]
        )

    def coming(self, t):
        return pltpu.make_async_copy(
            self.far.at[t], self.slot(self.back, t), self.sems.at[self.into + t]
        )

    def make_room(self, t):
        @pl.when(t >= self.SLOTS)
        def _():
            self.leaving(t - self.SLOTS).wait()

    def all_left(self):
        for t in range(self.count - self.SLOTS, self.count):
            self.leaving(t).wait()

    def open(self):
        for t in range(self.SLOTS):
            self.coming(t).start()

    def next(self, t):
        @pl.when(t + self.SLOTS < self.count)
        def _():
            self.coming(t + self.SLOTS).start()


class Place:
    def __init__(self, narrow):
        self.narrow = narrow
        wide = lax.axis_index("wide")
        self.z = lax.axis_index("narrow")
        self.y = wide // 4
        self.x = (wide // 2) % 2
        self.c = wide % 2
        self.other_y = 1 - self.y
        self.other_x = 1 - self.x
        self.other_c = 1 - self.c
        self.index = wide * narrow + self.z
        self.core_peer = (self.y * 4 + self.x * 2 + self.other_c, self.z)
        self.x_peer = (self.y * 4 + self.other_x * 2 + self.c, self.z)
        self.y_peer = (self.other_y * 4 + self.x * 2 + self.c, self.z)
        self.z_places = [lax.rem(self.z + k, narrow) for k in range(1, narrow)]
        self.z_from = [lax.rem(self.z + narrow - k, narrow) for k in range(1, narrow)]
        self.z_peers = [(wide, there) for there in self.z_places]

    def greet(self):
        barrier = pltpu.get_barrier_semaphore()
        peers = [self.core_peer, self.x_peer, self.y_peer] + self.z_peers
        for peer in peers:
            pl.semaphore_signal(barrier, inc=1, device_id=peer, device_id_type=MESH)
        return lambda: pl.semaphore_wait(barrier, len(peers))


class Gather:
    def __init__(self, at, shard, full, send, recv, number, copies):
        self.at, self.shard, self.full, self.copies = at, shard, full, copies
        self.send, self.recv, self.number = send, recv, number
        self.rows = shard.shape[0]
        self.half = shard.shape[0] * at.narrow // 2

    def copy(self, slot, source, target, peer):
        return pltpu.make_async_remote_copy(
            src_ref=source,
            dst_ref=target,
            send_sem=self.send.at[self.number, slot],
            recv_sem=self.recv.at[self.number, slot],
            device_id=peer,
            device_id_type=MESH,
        )

    def go(self, slot, region, peer, source=None):
        self.copy(slot, region if source is None else source, region, peer).start()

    def arrive(self, slot, region, peer):
        self.copy(slot, region, region, peer).wait_recv()

    def line(self, z):
        at = self.at
        rows = pl.ds(pl.multiple_of(z * self.rows, self.rows), self.rows)
        return self.full.at[at.y, at.x, at.c, rows]

    def begin(self):
        at = self.at
        for k in range(at.narrow - 1):
            self.go(k, self.line(at.z), at.z_peers[k], self.shard)
        self.own = self.copies.start(self.shard, self.line(at.z))

    def second(self):
        at, full, h = self.at, self.full, self.half
        self.copies.wait(self.own)
        for k in range(at.narrow - 1):
            self.arrive(k, self.line(at.z_from[k]), at.z_peers[k])
        n = at.narrow - 1
        self.go(n, full.at[at.y, at.x, at.c, pl.ds(0, h)], at.x_peer)
        self.go(n + 1, full.at[at.y, at.x, at.c, pl.ds(h, h)], at.y_peer)

    def third(self):
        at, full, h = self.at, self.full, self.half
        n = at.narrow - 1
        self.arrive(n, full.at[at.y, at.other_x, at.c, pl.ds(0, h)], at.x_peer)
        self.go(n + 2, full.at[at.y, :, at.c, pl.ds(0, h)], at.y_peer)
        self.arrive(n + 1, full.at[at.other_y, at.x, at.c, pl.ds(h, h)], at.y_peer)
        self.go(n + 3, full.at[:, at.x, at.c, pl.ds(h, h)], at.x_peer)

    def fourth(self):
        at, full, h = self.at, self.full, self.half
        n = at.narrow - 1
        self.arrive(n + 2, full.at[at.other_y, :, at.c, pl.ds(0, h)], at.y_peer)
        self.arrive(n + 3, full.at[:, at.other_x, at.c, pl.ds(h, h)], at.x_peer)
        self.go(n + 4, full.at[:, :, at.c], at.core_peer)

    def last(self):
        at, full = self.at, self.full
        self.arrive(at.narrow + 3, full.at[:, :, at.other_c], at.core_peer)

    def close(self):
        at, full, h, n = self.at, self.full, self.half, self.at.narrow - 1
        sent = [self.line(at.z)] * n
        sent += [full.at[at.y, at.x, at.c, pl.ds(0, h)], full.at[at.y, at.x, at.c, pl.ds(h, h)]]
        sent += [full.at[at.y, :, at.c, pl.ds(0, h)], full.at[:, at.x, at.c, pl.ds(h, h)]]
        sent += [full.at[:, :, at.c]]
        for slot, region in enumerate(sent):
            self.copy(slot, region, region, at.core_peer).wait_send()


class Scatter:
    SCRATCH = 6

    def __init__(self, at, grad, out, buffers, send, recv, number):
        self.at, self.grad, self.out = at, grad, out
        self.total, self.in_a, self.in_b, self.in_a2, self.in_b2, self.in_z = buffers
        self.send, self.recv, self.number = send, recv, number
        self.rows = out.shape[0]
        self.half = out.shape[0] * at.narrow // 2
    @staticmethod
    def scratch(rows, columns, narrow):
        block = rows * narrow
        h = block // 2
        return [
            pltpu.VMEM((2, 2, block, columns), BF16),
            pltpu.VMEM((2, h, columns), BF16),
            pltpu.VMEM((2, h, columns), BF16),
            pltpu.VMEM((h, columns), BF16),
            pltpu.VMEM((h, columns), BF16),
            pltpu.VMEM((narrow - 1, rows, columns), BF16),
        ]

    def copy(self, slot, source, target, peer):
        return pltpu.make_async_remote_copy(
            src_ref=source,
            dst_ref=target,
            send_sem=self.send.at[self.number, slot],
            recv_sem=self.recv.at[self.number, slot],
            device_id=peer,
            device_id_type=MESH,
        )

    def go(self, slot, source, target, peer):
        self.copy(slot, source, target, peer).start()

    def arrive(self, slot, target, peer):
        self.copy(slot, target, target, peer).wait_recv()

    def add(self, y, x, first, extra, index):
        size = 32

        def step(i):
            rows = pl.ds(pl.multiple_of(first + i * size, size), size)
            more = extra[(*index, pl.ds(pl.multiple_of(i * size, size), size))]
            made = self.total[y, x, rows, :].astype(F32) + more.astype(F32)
            self.total[y, x, rows, :] = made.astype(BF16)

        loop(extra.shape[-2] // size, step)

    def begin(self):
        at = self.at
        self.go(0, self.grad.at[:, :, at.other_c], self.total, at.core_peer)

    def second(self):
        at, h = self.at, self.half
        self.arrive(0, self.total, at.core_peer)
        loop(4, lambda t: self.add(t // 2, t % 2, 0, self.grad, (t // 2, t % 2, at.c)))
        self.go(1, self.total.at[at.other_y, :, pl.ds(0, h)], self.in_a, at.y_peer)
        self.go(2, self.total.at[:, at.other_x, pl.ds(h, h)], self.in_b, at.x_peer)

    def third(self):
        at, h = self.at, self.half
        self.arrive(1, self.in_a, at.y_peer)
        self.add(at.y, at.other_x, 0, self.in_a, (at.other_x,))
        self.go(3, self.total.at[at.y, at.other_x, pl.ds(0, h)], self.in_a2, at.x_peer)
        self.arrive(2, self.in_b, at.x_peer)
        self.add(at.other_y, at.x, h, self.in_b, (at.other_y,))
        self.go(4, self.total.at[at.other_y, at.x, pl.ds(h, h)], self.in_b2, at.y_peer)
        self.add(at.y, at.x, 0, self.in_a, (at.x,))
        self.add(at.y, at.x, h, self.in_b, (at.y,))

    def line(self, z):
        rows = pl.ds(pl.multiple_of(z * self.rows, self.rows), self.rows)
        return self.total.at[self.at.y, self.at.x, rows]

    def fourth(self):
        at, h = self.at, self.half
        self.arrive(3, self.in_a2, at.x_peer)
        self.add(at.y, at.x, 0, self.in_a2, ())
        self.arrive(4, self.in_b2, at.y_peer)
        self.add(at.y, at.x, h, self.in_b2, ())
        for k in range(at.narrow - 1):
            self.go(5 + k, self.line(at.z_places[k]), self.in_z.at[k], at.z_peers[k])

    def last(self):
        at = self.at
        rows = pl.ds(pl.multiple_of(at.z * self.rows, self.rows), self.rows)
        summed = self.total[at.y, at.x, rows, :].astype(F32)
        for k in range(at.narrow - 1):
            self.arrive(5 + k, self.in_z.at[k], at.z_peers[k])
            summed = summed + self.in_z[k].astype(F32)
        self.out[...] = summed

    def close(self):
        at, total, h = self.at, self.total, self.half
        sent = [self.grad.at[:, :, at.other_c]]
        sent += [total.at[at.other_y, :, pl.ds(0, h)], total.at[:, at.other_x, pl.ds(h, h)]]
        sent += [
            total.at[at.y, at.other_x, pl.ds(0, h)],
            total.at[at.other_y, at.x, pl.ds(h, h)],
        ]
        sent += [self.line(z) for z in at.z_places]
        for slot, region in enumerate(sent):
            self.copy(slot, region, region, at.core_peer).wait_send()


def unpack_vectors(vec_ref, full_ref, narrow):
    packed = matrix(full_ref)
    rows, lanes = packed.shape
    devices = rows // 16
    width = 512
    shape = (lanes, width)
    source = lax.broadcasted_iota(jnp.int32, shape, 0)
    place = lax.broadcasted_iota(jnp.int32, shape, 1)
    each = width // devices
    wide = (4 * width) // devices
    short = nn(packed, (source == place % each).astype(BF16))
    long = nn(packed, (source == place % wide).astype(BF16))
    shape = (rows, width)
    row = lax.broadcasted_iota(jnp.int32, shape, 0)
    lane = lax.broadcasted_iota(jnp.int32, shape, 1)
    short = jnp.where(row // 16 == lane // each, short, 0.0)
    kept = (row % 16 == IN_BIAS) & ((row // 16) % (devices // 4) == lane // wide)
    long = jnp.where(kept, long, 0.0)
    vec_ref[0:16, :] = jnp.sum(short.reshape(devices, 16, width), axis=0)
    for a in range(4):
        vec_ref[IN_BIAS + a : IN_BIAS + a + 1, :] = column_sum(
            long[a * rows // 4 : (a + 1) * rows // 4, :]
        )


WEIGHTS = 6
GATHERED = 9
SCATTERED = 5 + PAIRS
KEYS = 512
GROUP = 4
REACH = 3


def layer_kernel(exchange, narrow, *refs):
    refs = list(refs)
    take = lambda n: [refs.pop(0) for _ in range(n)]
    lengths, source_lengths, target_far, memory_far, cotangent_far = take(5)
    weights_far = take(WEIGHTS)
    if exchange:
        short_parts = take(6)
    else:
        (vec,) = take(1)
    output_far, memory_grad_far, target_grad_far = take(3)
    if exchange:
        outs = take(SCATTERED)
        (row_total,) = take(1)
    if exchange:
        self_far, cross_far = take(2)
        grads = take(4)
        (sums,) = take(1)
    else:
        grads = take(6)
        (sums,) = take(1)
        self_far, cross_far = take(2)
    weights = take(WEIGHTS)
    s_qkv, s_out, c_qkv, c_out, ff_in, ff_out = weights
    target, memory, cotangent, query, keys, values, mixed = take(7)
    cross_query, cross_key, cross_value, cross_mixed, hat, scale = take(6)
    turned, target_hit, source_hit, target_miss = take(4)
    activated, grad_pre_low, normed_low, low_three, low_two, grad_mixed, delta = take(7)
    portion, cross_portion, blocks, grad_blocks = take(4)
    grad, dk, dv, scale_two, local_sems = take(5)
    rows, width = target.shape
    if exchange:
        c_qkv_grad, c_out_grad, s_out_grad, s_parts = grads
        ff_out_grad, ff_in_grad = ff_out, ff_in
        grads = [ff_out_grad, ff_in_grad, c_qkv_grad, c_out_grad, s_out_grad]
        grads += [s_parts.at[n] for n in range(PAIRS)]
    else:
        ff_out_grad, ff_in_grad, c_qkv_grad, c_out_grad, s_out_grad, s_parts = grads
    sources = memory.shape[0]
    hidden = ff_in.shape[-1]
    steps = rows // TILE
    lines_count = rows // LINE
    copies = Copies(local_sems)
    self_kept = Kept(copies, self_far, activated, grad_pre_low)
    cross_kept = Kept(copies, cross_far, activated, grad_pre_low)

    if exchange:
        vec, short_full, short_wide, short, send, recv = take(6)
        buffers = [take(Scatter.SCRATCH) for _ in range(SCATTERED)]
        row_send, row_recv, s_send, s_recv, v_send, v_recv = take(6)
        at = Place(narrow)
        pairs = [(short, short_full)]
        for n in range(3):
            lanes = pl.ds(n * width, width)
            pairs.append((weights_far[0].at[:, lanes], s_qkv.at[:, :, :, :, lanes]))
        pairs += list(zip(weights_far[1:], weights[1:]))
        moves = [
            Gather(at, shard, full, send, recv, n, copies) for n, (shard, full) in enumerate(pairs)
        ]
        first, second, third = moves[0:4], moves[4:6], moves[6:9]
        sums_out = [
            Scatter(at, grads[n], outs[n], buffers[n], s_send, s_recv, n) for n in range(SCATTERED)
        ]
        ff_sum, cross_sum, out_sum = sums_out[0:2], sums_out[2:4], sums_out[4:5]
        part_sums = [sums_out[5 + n : 6 + n] for n in range(PAIRS)]

        def every(group, step):
            for move in group:
                getattr(move, step)()

        at_step = functools.partial(hook, every)
        all_here = at.greet()
        short_wide[...] = jnp.zeros_like(short_wide)
        row = 0
        for piece in short_parts:
            count, lanes = piece.shape
            short_wide[row : row + count, 0:lanes] = piece[...].astype(F32)
            row += count
        short[...] = short_wide[...].astype(BF16)
        all_here()
    else:
        first = second = third = ff_sum = cross_sum = out_sum = []
        part_sums = [[]] * PAIRS
        every = lambda group, step: None
        at_step = functools.partial(hook, None)

    every(first, "begin")
    loads = [copies.start(target_far, target)]
    later = [copies.start(memory_far, memory), copies.start(cotangent_far, cotangent)]
    if not exchange:
        for far_ref, near in zip(weights_far, weights):
            loads.append(copies.start(far_ref, near))
    hit = sentence_hits(lengths, rows)
    lane = lax.broadcasted_iota(jnp.int32, (rows, LINE), 1)
    target_hit[...] = jnp.where(hit, 1.0, 0.0).astype(BF16)
    target_miss[...] = jnp.where(hit | (lane >= lengths.shape[1]), 0.0, MASKED).astype(BF16)
    source_hit[...] = jnp.where(sentence_hits(source_lengths, sources), 1.0, 0.0).astype(BF16)
    sums[...] = jnp.zeros_like(sums)
    every(first, "second")
    every(second, "begin")
    every(first, "third")
    every(third, "begin")
    every(first, "fourth")
    every(second, "second")
    every(first, "last")
    if exchange:
        unpack_vectors(vec, short_full, narrow)
    copies.wait(*loads)

    def vector(row):
        return vec[row : row + 1, :]

    def add_sum(row, value):
        sums[row : row + 1, :] += column_sum(value)

    def project(i):
        lines = part(i, TILE)
        given = target[lines, :]
        made = nn(given, matrix(s_qkv, 0, width)) + vector(SELF_BIAS)
        query[lines, :] = (made * HEAD**-0.5).astype(BF16)
        keys[lines, :] = nn(given, matrix(s_qkv, width, width)).astype(BF16)
        made = nn(given, matrix(s_qkv, 2 * width, width)) + vector(SELF_BIAS + 1)
        low = made.astype(BF16)
        values[lines, :] = low
        turned[:, lines] = low.T

    each(steps, project)
    every(second, "third")
    every(third, "second")

    def query_block(ref, lines, lanes):
        missing = target_miss[lines, :]
        return beside(stacked(ref[lines, lanes]), jnp.concatenate([missing, missing], axis=0))

    def reach(i):
        return range(max(i - REACH + 1, 0), i + 1)

    def pair_lanes(pair):
        return pl.ds(pl.multiple_of(pair * PAIR, PAIR), PAIR)

    def rows_of(blocks_met):
        return slice(blocks_met[0] * LINE, (blocks_met[-1] + 1) * LINE)

    key_place = lax.broadcasted_iota(jnp.int32, (LINE, 2 * LINE), 0)
    query_place = lax.broadcasted_iota(jnp.int32, (LINE, 2 * LINE), 1) % LINE

    def attend(pair):
        lanes = pair_lanes(pair)
        self_kept.make_room(pair)
        for i in range(lines_count):
            lines, met = slice(i * LINE, (i + 1) * LINE), reach(i)
            span = rows_of(met)
            given = beside(keys[span, lanes], target_hit[span, :])
            scores = nt(given, query_block(query, lines, lanes))
            last = (len(met) - 1) * LINE
            pieces = [jnp.where(key_place <= query_place, scores[last:], MASKED)]
            if last:
                pieces.insert(0, scores[:last])
            tops = [jnp.max(value, axis=0, keepdims=True) for value in pieces]
            top = functools.reduce(jnp.maximum, tops)
            pieces = [jnp.exp(value - top) for value in pieces]
            by = 1.0 / sum(column_sum(value) for value in pieces)
            exponent = jnp.concatenate([value.astype(BF16) for value in pieces], axis=0)
            for n, k in enumerate(met):
                place = self_kept.place(pair, i - k)
                activated[k * LINE : (k + 1) * LINE, place] = exponent[n * LINE : (n + 1) * LINE]
            made = diagonal(nn(turned[lanes, span], exponent)) * spread_rows(by)
            mixed[lines, lanes] = made.T.astype(BF16)
            keep_row(portion, i, pair, by)
        self_kept.leaving(pair).start()

    loop(PAIRS, attend, at_step(0, (second, "fourth")) + at_step(1, (third, "third")))
    self_kept.all_left()
    every(second, "last")
    copies.wait(*later)

    def close_self(i):
        lines = part(i, TILE)
        summed = target[lines, :].astype(F32) + nn(mixed[lines, :], matrix(s_out))
        made, by = normalise(summed + vector(SELF_BIAS + 2))
        hat[lines, :] = made
        scale[lines, :] = jnp.broadcast_to(by, (TILE, LINE))
        normed = (made * vector(GAIN) + vector(SHIFT)).astype(BF16)
        made = nn(normed, matrix(c_qkv, 0, width)) + vector(CROSS_BIAS)
        cross_query[lines, :] = (made * HEAD**-0.5).astype(BF16)
        given = memory[lines, :]
        cross_key[lines, :] = nn(given, matrix(c_qkv, width, width)).astype(BF16)
        made = nn(given, matrix(c_qkv, 2 * width, width)) + vector(CROSS_BIAS + 1)
        low = made.astype(BF16)
        cross_value[lines, :] = low
        turned[:, lines] = low.T

    each(steps, close_self)

    groups = lines_count // GROUP
    cross_steps = PAIRS * groups

    def attend_cross(t):
        pair, group = t // groups, t % groups
        lanes = pair_lanes(pair)
        cross_kept.make_room(t)
        for n in range(GROUP):
            i = group * GROUP + n
            lines = part(i, LINE)
            block = query_block(cross_query, lines, lanes)
            scores = []
            for c in range(sources // KEYS):
                span = slice(c * KEYS, (c + 1) * KEYS)
                scores.append(nt(beside(cross_key[span, lanes], source_hit[span, :]), block))
            tops = [jnp.max(value, axis=0, keepdims=True) for value in scores]
            top = functools.reduce(jnp.maximum, tops)
            exponents = [jnp.exp(value - top) for value in scores]
            by = 1.0 / sum(column_sum(value) for value in exponents)
            exponent = jnp.concatenate([value.astype(BF16) for value in exponents], axis=0)
            activated[:, cross_kept.place(t, n)] = exponent
            made = diagonal(nn(turned[lanes, :], exponent)) * spread_rows(by)
            cross_mixed[lines, lanes] = made.T.astype(BF16)
            keep_row(cross_portion, i, pair, by)
        cross_kept.leaving(t).start()

    loop(cross_steps, attend_cross, at_step(cross_steps // 2 - 1, (third, "fourth")))
    cross_kept.all_left()
    every(third, "last")

    hat_two, slope = dk, grad_pre_low
    parts = hidden // CHUNK

    def open_feed(i):
        lines = part(i, TILE)
        normed_one = hat[lines, :] * vector(GAIN) + vector(SHIFT)
        summed = normed_one + nn(cross_mixed[lines, :], matrix(c_out)) + vector(CROSS_BIAS + 2)
        made, by = normalise(summed)
        hat_two[lines, :] = made
        scale_two[lines, :] = jnp.broadcast_to(by, (TILE, LINE))
        normed_low[lines, :] = (made * vector(GAIN + 1) + vector(SHIFT + 1)).astype(BF16)

    def feed_in(j, i):
        lines, lanes = part(i, TILE), part(j, CHUNK)
        weight = ff_in[:, :, :, :, lanes].reshape(width, CHUNK)
        u = nn(normed_low[lines, :], weight) + vec[pl.ds(IN_BIAS + j, 1), :]
        c0 = math.sqrt(2.0 / math.pi)
        square = u * u
        rise = 0.5 + 0.5 * jnp.tanh(u * (c0 + (c0 * 0.044715) * square))
        made = u * rise
        activated[lines, lanes] = made.astype(BF16)
        rate = rise + made * (1.0 - rise) * (2.0 * c0 + (6.0 * c0 * 0.044715) * square)
        slope[lines, lanes] = rate.astype(BF16)

    def feed_out(i):
        lines = part(i, TILE)
        normed_two = hat_two[lines, :] * vector(GAIN + 1) + vector(SHIFT + 1)
        summed = normed_two + nn(activated[lines, :], matrix(ff_out)) + vector(OUT_BIAS)
        hat_three, scale_three = normalise(summed)
        given = cotangent[lines, :].astype(F32)
        cotangent[lines, :] = (hat_three * vector(GAIN + 2) + vector(SHIFT + 2)).astype(BF16)
        add_sum(GAIN + 2, given * hat_three)
        add_sum(SHIFT + 2, given)
        grad_three = normalise_back(given, hat_three, scale_three, vector(GAIN + 2))
        add_sum(OUT_BIAS, grad_three)
        low_three[lines, :] = grad_three.astype(BF16)
        grad[lines, :] = grad_three

    def back_out(j, i):
        lines, lanes = part(i, TILE), part(j, CHUNK)
        weight = ff_out[j // 2, j % 2].reshape(CHUNK, width)
        grad_pre = nt(low_three[lines, :], weight) * slope[lines, lanes].astype(F32)
        sums[pl.ds(IN_BIAS + j, 1), :] += column_sum(grad_pre)
        grad_pre_low[lines, lanes] = grad_pre.astype(BF16)

    def back_in(i):
        lines = part(i, TILE)
        given = grad[lines, :] + nt(grad_pre_low[lines, :], matrix(ff_in))
        made = hat_two[lines, :]
        add_sum(GAIN + 1, given * made)
        add_sum(SHIFT + 1, given)
        grad_two = normalise_back(given, made, scale_two[lines, 0:1], vector(GAIN + 1))
        add_sum(CROSS_BIAS + 2, grad_two)
        grad[lines, :] = grad_two
        low = grad_two.astype(BF16)
        low_two[lines, :] = low
        mixed_grad = nt(low, matrix(c_out)).astype(BF16)
        write_grad(grad_mixed, delta, cross_portion, i, mixed_grad, cross_mixed[lines, :])

    if exchange:
        for move in moves:
            move.close()
    each(steps, open_feed)
    loop(parts, lambda j: each(steps, functools.partial(feed_in, j)))
    loop(steps, feed_out)
    copies.start(cotangent, output_far)
    loop(parts, lambda j: each(steps, functools.partial(back_out, j)))
    weight_grad(ff_out_grad, activated, low_three)
    every(ff_sum[:1], "begin")
    loop(steps, back_in)
    weight_grad(ff_in_grad, normed_low, grad_pre_low)
    every(ff_sum[1:], "begin")
    weight_grad(c_out_grad, cross_mixed, low_two)
    every(cross_sum[1:], "begin")

    dq = activated.at[:, 0:width]
    cross_dk_low, cross_dv_low = normed_low, cross_mixed
    cross_kept.open()

    def clear(i):
        lines = part(i, TILE)
        dk[lines, :] = jnp.zeros((TILE, width), F32)
        dv[lines, :] = jnp.zeros((TILE, width), F32)

    def turn(ref):
        def step(i):
            lines = part(i, TILE)
            turned[:, lines] = ref[lines, :].T

        return step

    loop(steps, clear)
    loop(steps, turn(cross_key))
    every(ff_sum, "second")

    grad_scores = activated.at[:, 2 * width : 4 * width]

    def attend_cross_back(t):
        pair, group = t // groups, t % groups
        lanes = pair_lanes(pair)
        places = [slice(n * 2 * LINE, (n + 1) * 2 * LINE) for n in range(GROUP)]
        for n, place in enumerate(places):
            lines = part(group * GROUP + n, LINE)
            blocks[place, :] = stacked(cross_query[lines, lanes])
            grad_blocks[place, :] = stacked(grad_mixed[lines, lanes])
        cross_kept.coming(t).wait()

        def some_keys(c):
            span = slice(c * KEYS, (c + 1) * KEYS)
            for n, place in enumerate(places):
                grad_scores[span, place] = score_back(
                    grad_pre_low[span, cross_kept.place(t, n)],
                    cross_value[span, lanes],
                    grad_blocks[place, :],
                    pair_row(delta, group * GROUP + n, pair),
                )
            kept = grad_pre_low[span, cross_kept.place(t, 0, cross_kept.lanes)]
            dv[span, lanes] += nn(kept, grad_blocks[0 : cross_kept.lanes, :])
            dk[span, lanes] += nn(grad_scores[span, :], blocks[0 : cross_kept.lanes, :])

        for c in range(sources // KEYS):
            some_keys(c)
        for n, place in enumerate(places):
            made = diagonal(nn(turned[lanes, :], grad_scores[:, place])).T * HEAD**-0.5
            sums[CROSS_BIAS : CROSS_BIAS + 1, lanes] += column_sum(made)
            dq[part(group * GROUP + n, LINE), lanes] = made.astype(BF16)
        cross_kept.next(t)

    loop(
        cross_steps,
        attend_cross_back,
        at_step(cross_steps // 4, (ff_sum, "third"))
        + at_step(cross_steps * 5 // 8, (cross_sum[1:], "second"), (ff_sum, "fourth")),
    )
    every(cross_sum[1:], "third")

    def close_cross(i):
        lines = part(i, TILE)
        made = dv[lines, :]
        add_sum(CROSS_BIAS + 1, made)
        cross_dv_low[lines, :] = made.astype(BF16)
        cross_dk_low[lines, :] = dk[lines, :].astype(BF16)
        low_three[lines, :] = (hat[lines, :] * vector(GAIN) + vector(SHIFT)).astype(BF16)

    self_kept.open()
    each(steps, close_cross)
    weight_grad(c_qkv_grad, low_three, dq, 0)
    weight_grad(c_qkv_grad, memory, cross_dk_low, width)
    weight_grad(c_qkv_grad, memory, cross_dv_low, 2 * width)
    every(cross_sum[:1], "begin")
    every(cross_sum[1:], "fourth")

    def open_self(i):
        lines = part(i, TILE)
        given = grad[lines, :] + nt(dq[lines, :], matrix(c_qkv, 0, width))
        made = hat[lines, :]
        add_sum(GAIN, given * made)
        add_sum(SHIFT, given)
        grad_one = normalise_back(given, made, scale[lines, 0:1], vector(GAIN))
        add_sum(SELF_BIAS + 2, grad_one)
        grad[lines, :] = grad_one
        low = grad_one.astype(BF16)
        low_two[lines, :] = low
        mixed_grad = nt(low, matrix(s_out)).astype(BF16)
        write_grad(grad_mixed, delta, portion, i, mixed_grad, mixed[lines, :])
        turned[:, lines] = keys[lines, :].T

    each(steps, open_self)
    every(cross_sum[:1], "second")
    weight_grad(s_out_grad, mixed, low_two)
    every(out_sum, "begin")
    all_grads = activated.at[:, 0 : 3 * width]

    def score_place(k, n):
        rows_here = slice(k * LINE, (k + 1) * LINE)
        if n < 2:
            return low_three.at[rows_here, n * 2 * LINE : (n + 1) * 2 * LINE]
        return low_two.at[rows_here, 0 : 2 * LINE]

    def attend_back(pair):
        lanes = pair_lanes(pair)

        def own(n):
            return pl.ds(pl.multiple_of(pair * 3 * PAIR + n * PAIR, PAIR), PAIR)

        for i in range(lines_count):
            lines = slice(i * LINE, (i + 1) * LINE)
            place = slice(i * 2 * LINE, (i + 1) * 2 * LINE)
            blocks[place, :] = stacked(query[lines, lanes])
            grad_blocks[place, :] = stacked(grad_mixed[lines, lanes])
        less = [pair_row(delta, i, pair) for i in range(lines_count)]
        self_kept.coming(pair).wait()
        value_sum = jnp.zeros((1, PAIR), F32)
        for k in range(lines_count):
            lines = slice(k * LINE, (k + 1) * LINE)
            count = min(REACH, lines_count - k)
            place = slice(k * 2 * LINE, (k + count) * 2 * LINE)
            exponent = grad_pre_low[lines, self_kept.place(pair, 0, count * 2 * LINE)]
            block, grad_block = blocks[place, :], grad_blocks[place, :]
            grad_score = score_back(
                exponent,
                values[lines, lanes],
                grad_block,
                jnp.concatenate(less[k : k + count], axis=1),
            )
            for n in range(count):
                score_place(k, n)[...] = grad_score[:, n * 2 * LINE : (n + 1) * 2 * LINE]
            made = nn(exponent, grad_block)
            value_sum = value_sum + column_sum(made)
            all_grads[lines, own(2)] = made.astype(BF16)
            all_grads[lines, own(1)] = nn(grad_score, block).astype(BF16)
        sums[SELF_BIAS + 1 : SELF_BIAS + 2, lanes] += value_sum
        for i in range(lines_count):
            met = reach(i)
            grad_score = jnp.concatenate([score_place(k, i - k)[...] for k in met], axis=0)
            made = diagonal(nn(turned[lanes, rows_of(met)], grad_score)).T * HEAD**-0.5
            sums[SELF_BIAS : SELF_BIAS + 1, lanes] += column_sum(made)
            all_grads[i * LINE : (i + 1) * LINE, own(0)] = made.astype(BF16)
        self_kept.next(pair)
        weight_grad(s_parts.at[pair], target, all_grads, 0, pair * 3 * PAIR, 3 * PAIR)
        for n in range(PAIRS):
            pl.when(pair == n)(functools.partial(every, part_sums[n], "begin"))

    loop(
        PAIRS,
        attend_back,
        at_step(0, (cross_sum[:1], "third"), (out_sum, "second"))
        + at_step(1, (cross_sum[:1], "fourth"), (out_sum, "third"), (part_sums[0], "second"))
        + at_step(2, (out_sum, "fourth"), (part_sums[0], "third"), (part_sums[1], "second"))
        + at_step(3, (part_sums[0], "fourth"), (part_sums[1], "third"), (part_sums[2], "second")),
    )

    row_moves = []
    row_moves = []
    row_moves = []

    def row_copy(slot, stage, peer):
        return pltpu.make_async_remote_copy(
            src_ref=row_send.at[stage],
            dst_ref=row_recv.at[slot],
            send_sem=v_send.at[slot],
            recv_sem=v_recv.at[slot],
            device_id=peer,
            device_id_type=MESH,
        )

    def row_go(slots, stage, peers):
        for slot, peer in zip(slots, peers):
            moving = row_copy(slot, stage, peer)
            moving.start()
            row_moves.append((slot, moving))

    def row_add(slots, stage):
        total = row_send[stage]
        for slot, moving in row_moves:
            if slot in slots:
                moving.wait_recv()
                total = total + row_recv[slot]
        return total

    if exchange:
        row_send[0] = sums[...]
        row_go([0], 0, [at.core_peer])
    final = copies.tiles(grad, target_grad_far, steps, TILE)
    memory_final = copies.tiles(dk, memory_grad_far, sources // TILE, TILE)

    def close(i):
        lines = part(i, TILE)
        made = grad[lines, :]
        for k in range(3):
            places = [(3 * p + k) * PAIR for p in range(PAIRS)]
            left = jnp.concatenate([all_grads[lines, a : a + PAIR] for a in places], axis=1)
            made = made + nt(left, matrix(s_qkv, k * width, width))
        grad[lines, :] = made
        final.start(i)

    def close_memory(i):
        lines = part(i, TILE)
        dk[lines, :] = nt(cross_dk_low[lines, :], matrix(c_qkv, width, width)) + nt(
            cross_dv_low[lines, :], matrix(c_qkv, 2 * width, width)
        )
        memory_final.start(i)

    loop(
        sources // TILE,
        close_memory,
        at_step(0, (part_sums[3], "second"), (part_sums[1], "fourth"))
        + at_step(1, (part_sums[2], "third")),
    )
    if exchange:
        row_send[1] = row_add([0], 0)
        row_go([1], 1, [at.x_peer])
    loop(steps, close, at_step(0, (part_sums[3], "third"), (part_sums[2], "fourth")))
    if exchange:
        row_send[2] = row_add([1], 1)
        row_go([2], 2, [at.y_peer])
    every(ff_sum, "last")
    every(cross_sum, "last")
    every(out_sum, "last")
    every(part_sums[3], "fourth")
    if exchange:
        slots = list(range(3, narrow + 2))
        row_send[3] = row_add([2], 2)
        row_go(slots, 3, at.z_peers)
    for group in part_sums:
        every(group, "last")
    if exchange:
        row_total[...] = row_add(slots, 3)
        for move in sums_out:
            move.close()
        for _, moving in row_moves:
            moving.wait_send()
    final.wait_all()
    memory_final.wait_all()
    copies.close()


def tail_kernel(narrow, *refs):
    refs = list(refs)
    take = lambda n: [refs.pop(0) for _ in range(n)]
    far_in = take(3 + 1 + SCATTERED)
    far_out = take(3 + WEIGHTS)
    s_bias, c_bias, gain_out, shift_out, in_bias, out_bias = take(6)
    near = take(3 + 1 + SCATTERED)
    joined, sems = take(2)
    copies = Copies(sems)
    wide = []
    piece = TILE // 2
    for source, buffer, out in zip(far_in[:3], near[:3], far_out[:3]):
        steps = buffer.shape[0] // piece
        entering = copies.tiles(source, buffer, steps, piece)
        entering.start_all()
        wide.append((steps, entering, copies.tiles(buffer, out, steps, piece)))
    plain = [copies.start(source, buffer) for source, buffer in zip(far_in[3:], near[3:])]
    for steps, entering, leaving in wide:
        for i in range(steps):
            entering.wait(i)
            leaving.start(i)
    copies.wait(*plain)
    for buffer, out in zip(near[4:9], far_out[3:8]):
        copies.start(buffer, out)
    for p, source in enumerate(near[9:]):
        for k in range(3):
            lanes = slice((k * PAIRS + p) * PAIR, (k * PAIRS + p + 1) * PAIR)
            joined[:, lanes] = source[:, k * PAIR : (k + 1) * PAIR]
    copies.start(joined, far_out[8])
    total = near[3][...]
    width = total.shape[1]
    devices = 8 * narrow
    index = lax.axis_index("wide") * narrow + lax.axis_index("narrow")
    each = width // devices
    own = pltpu.roll(total, lax.rem(width - index * each, width), 1)
    s_bias[...] = own[SELF_BIAS : SELF_BIAS + 3, :each]
    c_bias[...] = own[CROSS_BIAS : CROSS_BIAS + 3, :each]
    gain_out[...] = own[GAIN : GAIN + 3, :each]
    shift_out[...] = own[SHIFT : SHIFT + 3, :each]
    out_bias[...] = own[OUT_BIAS : OUT_BIAS + 1, :each]
    long = 4 * each
    in_row = devices // 4
    own = pltpu.roll(total, lax.rem(width - lax.rem(index, in_row) * long, width), 1)
    row = lax.broadcasted_iota(jnp.int32, own.shape, 0)
    own = column_sum(jnp.where(row == IN_BIAS + index // in_row, own, 0.0))
    in_bias[...] = own[:, :long]
    for _, _, leaving in wide:
        leaving.wait_all()
    copies.close()


def shape(dims, dtype):
    return jax.ShapeDtypeStruct(tuple(dims), dtype)


def whole(count):
    return [pl.BlockSpec(memory_space=pltpu.VMEM)] * count


def far(count):
    return [pl.BlockSpec(memory_space=pl.ANY)] * count


def scalars(count):
    return [pl.BlockSpec(memory_space=pltpu.SMEM)] * count


def cut(rows, columns):
    return (2, 2, 2, rows // 8, columns)


def local(wide, narrow, *args):
    target, memory, cotangent, target_lengths, source_lengths = args[:5]
    self_qkv, self_out, self_bias, cross_qkv, cross_out, cross_bias = args[5:11]
    ff_in, ff_in_bias, ff_out, ff_out_bias, ln_gain, ln_bias = args[11:]
    rows, width = target.shape
    sources = memory.shape[0]
    hidden = ff_in.shape[1]
    lines = rows // LINE
    axes = ("wide", "narrow")
    exchange = wide == 8 and narrow == 4 and self_qkv.shape[0] % 16 == 0
    weights = [self_qkv, self_out, cross_qkv, cross_out, ff_in, ff_out]

    def params(number):
        if exchange and number is not None:
            return pltpu.CompilerParams(
                collective_id=number, has_side_effects=True, vmem_limit_bytes=VMEM_BYTES
            )
        return pltpu.CompilerParams(vmem_limit_bytes=VMEM_BYTES)

    wide_outs = [
        shape((rows, width), BF16),
        shape((sources, width), F32),
        shape((rows, width), F32),
    ]
    table = shape((VECTORS, width), F32)
    partial_sums = [
        shape(cut(hidden, width), BF16),
        shape(cut(width, hidden), BF16),
        shape(cut(width, 3 * width), BF16),
        shape(cut(width, width), BF16),
        shape(cut(width, width), BF16),
        shape((PAIRS,) + cut(width, 3 * width // PAIRS), BF16),
        table,
    ]
    row_block = shape((rows, width), BF16)
    source_block = shape((sources, width), BF16)
    row_sums = shape((lines, HEADS, LINE), F32)
    scratch = [shape(cut(w.shape[0] * wide * narrow, w.shape[1]), BF16) for w in weights]
    scratch += [row_block, source_block] + [row_block] * 5
    scratch += [row_block, source_block, source_block, row_block]
    scratch += [shape((rows, width), F32), shape((rows, LINE), F32)]
    scratch += [
        shape((width, rows), BF16),
        shape((rows, LINE), BF16),
        shape((sources, LINE), BF16),
        shape((rows, LINE), BF16),
        shape((rows, hidden), BF16),
        shape((rows, hidden), BF16),
        row_block,
        row_block,
        row_block,
        row_block,
        row_sums,
        row_sums,
        row_sums,
        shape((2 * rows, PAIR), BF16),
        shape((2 * rows, PAIR), BF16),
        shape((rows, width), F32),
        shape((sources, width), F32),
        shape((sources, width), F32),
        shape((rows, LINE), F32),
    ]
    outs = list(wide_outs)
    if exchange:
        shorts = [self_bias, cross_bias, ln_gain, ln_bias]
        shorts += [ff_out_bias[None, :], ff_in_bias[None, :]]
        given = weights + shorts
        specs = far(len(weights)) + whole(len(shorts))
        own = [ff_out, ff_in, cross_qkv, cross_out, self_out]
        outs += [shape(w.shape, F32) for w in own]
        outs += [shape((self_qkv.shape[0], 3 * width // PAIRS), F32)] * PAIRS
        scattered = outs[3:]
        outs.append(table)
        scratch = partial_sums[2:] + scratch
    else:
        gathered = [lax.all_gather(w, axes, axis=0, tiled=True) for w in weights]
        short_rows = [self_bias, cross_bias, ln_gain, ln_bias, ff_out_bias[None, :]]
        vec = jnp.concatenate(
            [lax.all_gather(v, axes, axis=1, tiled=True) for v in short_rows], axis=0
        )
        last = lax.all_gather(ff_in_bias, axes, axis=0, tiled=True).reshape(-1, width)
        vec = jnp.concatenate([vec, last], axis=0).astype(F32)
        vec = jnp.pad(vec, ((0, VECTORS - vec.shape[0]), (0, 0)))
        given = [w.reshape(cut(*w.shape)) for w in gathered] + [vec]
        specs = far(len(weights)) + whole(1)
        outs += partial_sums
    outs.append(shape((PAIRS, rows, REACH * 2 * LINE), BF16))
    outs.append(shape((PAIRS * lines // GROUP, sources, GROUP * 2 * LINE), BF16))
    buffers = [pltpu.VMEM(x.shape, x.dtype) for x in scratch]
    buffers.append(pltpu.SemaphoreType.DMA((Copies.COUNT,)))
    if exchange:
        buffers += [
            pltpu.VMEM((VECTORS, width), F32),
            pltpu.VMEM(cut(16 * wide * narrow, 256), BF16),
            pltpu.VMEM((16, 256), F32),
            pltpu.VMEM((16, 256), BF16),
        ]
        buffers += [pltpu.SemaphoreType.DMA((GATHERED, narrow + 4))] * 2
        for w in scattered:
            buffers += Scatter.scratch(w.shape[0], w.shape[1], narrow)
        buffers += [
            pltpu.VMEM((4, VECTORS, width), F32),
            pltpu.VMEM((narrow + 2, VECTORS, width), F32),
        ]
        buffers += [pltpu.SemaphoreType.DMA((SCATTERED, narrow + 4))] * 2
        buffers += [pltpu.SemaphoreType.DMA((narrow + 2,))] * 2
    made = pl.pallas_call(
        functools.partial(layer_kernel, exchange, narrow),
        out_shape=outs,
        in_specs=scalars(2) + far(3) + specs,
        out_specs=far(3) + whole(len(outs) - 5) + far(2),
        scratch_shapes=buffers,
        compiler_params=params(0),
        name="layer",
    )(target_lengths, source_lengths, target, memory, cotangent, *given)
    if exchange:
        own.append(self_qkv)
        outs = wide_outs + [shape(w.shape, F32) for w in own]
        outs += [
            shape(self_bias.shape, F32),
            shape(cross_bias.shape, F32),
            shape(ln_gain.shape, F32),
            shape(ln_bias.shape, F32),
            shape((1, ff_in_bias.shape[0]), F32),
            shape((1, ff_out_bias.shape[0]), F32),
        ]
        made = pl.pallas_call(
            functools.partial(tail_kernel, narrow),
            out_shape=outs,
            in_specs=far(4 + SCATTERED),
            out_specs=far(3 + WEIGHTS) + whole(6),
            scratch_shapes=[
                pltpu.VMEM(x.shape, x.dtype) for x in wide_outs + [table] + scattered
            ]
            + [pltpu.VMEM(self_qkv.shape, F32), pltpu.SemaphoreType.DMA((Copies.COUNT,))],
            compiler_params=params(None),
            name="tail",
        )(*made[:3], made[3 + SCATTERED], *made[3 : 3 + SCATTERED])
    output, memory_grad, target_grad = made[:3]
    if exchange:
        f_out_sum, f_in_sum, c_qkv_sum, c_out_sum, s_out_sum, s_qkv_sum = made[3:9]
        s_bias_sum, c_bias_sum, gain_sum, shift_sum, in_bias_sum, out_bias_sum = made[9:]
        in_bias_sum = in_bias_sum.reshape(-1)
        out_bias_sum = out_bias_sum.reshape(-1)
    else:

        def spread(value):
            value = value.reshape(-1, value.shape[-1]).astype(F32)
            return lax.psum_scatter(value, axes, scatter_dimension=0, tiled=True)

        def spread_row(value):
            return lax.psum_scatter(value, axes, scatter_dimension=value.ndim - 1, tiled=True)

        f_out_sum, f_in_sum, c_qkv_sum, c_out_sum, s_out_sum = [spread(v) for v in made[3:8]]
        pieces = [spread(made[8][n]).reshape(-1, 3, width // PAIRS) for n in range(PAIRS)]
        s_qkv_sum = jnp.concatenate(pieces, axis=2).reshape(-1, 3 * width)
        sums = made[9]
        s_bias_sum = spread_row(sums[SELF_BIAS : SELF_BIAS + 3])
        c_bias_sum = spread_row(sums[CROSS_BIAS : CROSS_BIAS + 3])
        gain_sum = spread_row(sums[GAIN : GAIN + 3])
        shift_sum = spread_row(sums[SHIFT : SHIFT + 3])
        out_bias_sum = spread_row(sums[OUT_BIAS])
        in_bias_sum = spread_row(sums[IN_BIAS : IN_BIAS + hidden // width].reshape(-1))
    return (
        output,
        target_grad,
        memory_grad,
        s_qkv_sum,
        s_out_sum,
        s_bias_sum,
        c_qkv_sum,
        c_out_sum,
        c_bias_sum,
        f_in_sum,
        in_bias_sum,
        f_out_sum,
        out_bias_sum,
        gain_sum,
        shift_sum,
    )


def solution(mesh):
    rows = P(("wide", "narrow"), None)
    columns = P(None, ("wide", "narrow"))
    flat = P(("wide", "narrow"))
    return jax.shard_map(
        functools.partial(local, mesh.shape["wide"], mesh.shape["narrow"]),
        mesh=mesh,
        in_specs=(
            rows,
            rows,
            rows,
            rows,
            rows,
            rows,
            rows,
            columns,
            rows,
            rows,
            columns,
            rows,
            flat,
            rows,
            flat,
            columns,
            columns,
        ),
        out_specs=(
            rows,
            rows,
            rows,
            rows,
            rows,
            columns,
            rows,
            rows,
            columns,
            rows,
            flat,
            rows,
            flat,
            columns,
            columns,
        ),
        check_vma=False,
    )
```

time: 2230 us -> 181 us (0.08)
  waiting for transfers between devices: 1060 us -> 0 us
  matrix products: 493 us -> 0 us
  blocking collectives: 490 us -> 0 us
  Pallas kernels: 0 us -> 180 us
  local copies, waits for them, and re-layouts: 109 us -> 0 us
  other arithmetic: 53.3 us -> 0 us
    reduce_scatter x4 -> x0, waiting for transfers between devices: 567 us -> none  [the longest x1 150 us: local(): lax.psum_scatter(f_out_grad, ('wide', 'narrow'), scatter_dimension=0, til...]
    dot_general x245 -> x0, matrix products: 493 us -> none  [the longest x71 145 us: contract_rows(): lax.dot_general(left_side, right_side, (((0,), (0,)), ((), ())), preferre...]
    unnamed x20 -> x0, waiting for transfers between devices: 488 us -> none
    all_gather x6 -> x0, blocking collectives: 412 us -> none  [the longest x1 74.3 us: local(): lax.all_gather(cross_out, ('wide', 'narrow'), axis=0, tiled=True)]
    pallas_call x0 -> x2, Pallas kernels: none -> 180 us  [the longest x1 174 us: local(): pl.pallas_call(functools.partial(layer_kernel, exchange, narrow), out_sha...]
    unnamed x2 -> x0, blocking collectives: 78.3 us -> none
    unnamed x175 -> x0, local copies, waits for them, and re-layouts: 57.2 us -> none
    reduce_sum x48 -> x0, other arithmetic: 29.2 us -> none  [the longest x32 15.3 us: one_head(): row_total = jnp.sum(exponent, axis=1, keepdims=True)]
  transfers between devices with their start and end apart: 14 -> 0, of which waited for: 9 -> 0; matrix products, arithmetic and copies ran while one was open for 20% -> 0% of each run, Pallas kernels for 0% -> 0%
where the time goes in v1:
time: 181 us
  Pallas kernels  180 us (99%)
    pallas_call x1, Pallas kernels, local(): pl.pallas_call(functools.partial(layer_kernel, exchange, narrow), out_sha...  174 us
    pallas_call x1, Pallas kernels, local(): pl.pallas_call(functools.partial(tail_kernel, narrow), out_shape=outs, in...  6.6 us

profile of v1, /device:TPU:0, one launch (start us, length us, event | category | flops | bytes accessed | tf_op | source)
XLA Modules:
  0.0 181.1 jit_solution(9007816556232740282)
XLA Ops:
  0.7 173.6 %layer.1 = (bf16[1024,512]{1,0:T(8,128)(2,1)}, f32[1024,512]{1,0:T(8,128)}, f32[1024,512]{1,0:T(8,128)}, f32[64,512]{1,0:T(8,128)}, f32[16,2048]{1,0:T(8,128)}, ...) custom-call(s32[1,27]{1,0:T(1,128)} %refs_0_.1, ...), custom_call_target="tpu_custom_call" | custom-call | tf_op jit(solution)/shard_map/layer/pallas_call | solution.py:1254
  174.3 6.6 %tail.1 = (bf16[1024,512]{1,0:T(8,128)(2,1)}, f32[1024,512]{1,0:T(8,128)}, f32[1024,512]{1,0:T(8,128)}, f32[64,512]{1,0:T(8,128)}, f32[16,2048]{1,0:T(8,128)}, /...) custom-call(bf16[1024,512]{1,0:T(8,128)(2,1)} %get-tuple-element.43., ...), custom_call_target="tpu_custom_call" | custom-call | tf_op jit(solution)/shard_map/tail/pallas_call | solution.py:1274
